TPU v7x, 32 devices: a whole 2x2x4 slice. The times are simulated.
32 devices in a mesh: img: 16 (over z, y, x), pix: 2 (over core).
Axes of the slice: x: 2, y: 2, z: 4, core: 2. Of those that a mesh axis runs over, the one named last changes fastest.
Arguments:
- images_in: bfloat16 [16, 32, 32, 384], P('img', 'pix'), may hold values from -6 to 6
- extents: int32 [16, 2], P('img'), may hold values from 8 to 32, as said below
- timesteps: int32 [16], P('img'), may hold values from 0 to 39
- gain_first: float32 [384], replicated, may hold values from 0.5 to 1.5
- shift_first: float32 [384], replicated, may hold values from -1.8 to 1.8
- kernel_first: bfloat16 [3, 3, 384, 384], replicated, may hold values from -0.109375 to 0.109375
- offset_first: float32 [384], replicated, may hold values from -1.8 to 1.8
- embed_weight: bfloat16 [768, 768], replicated, may hold values from -0.21875 to 0.21875
- embed_offset: float32 [768], replicated, may hold values from -1.8 to 1.8
- gain_second: float32 [384], replicated, may hold values from 0.5 to 1.5
- shift_second: float32 [384], replicated, may hold values from -1.8 to 1.8
- kernel_second: bfloat16 [3, 3, 384, 384], replicated, may hold values from -0.15625 to 0.15625
- offset_second: float32 [384], replicated, may hold values from -1.8 to 1.8
- gain_attend: float32 [384], replicated, may hold values from 0.5 to 1.5
- shift_attend: float32 [384], replicated, may hold values from -1.8 to 1.8
- project_in: bfloat16 [384, 1152], replicated, may hold values from -0.3125 to 0.3125
- offset_in: float32 [768], replicated, may hold values from -1.8 to 1.8
- project_out: bfloat16 [384, 384], replicated, may hold values from -3.5 to 3.5
- offset_out: float32 [384], replicated, may hold values from -1.8 to 1.8
- out_grad: bfloat16 [16, 32, 32, 384], P('img', 'pix'), may hold values from -6 to 6
Outputs:
- result: bfloat16 [16, 32, 32, 384], P('img', 'pix')
- in_grad: bfloat16 [16, 32, 32, 384], P('img', 'pix')
- grad_gain_first: float32 [384], replicated
- grad_shift_first: float32 [384], replicated
- grad_kernel_first: float32 [3, 3, 384, 384], replicated
- grad_offset_first: float32 [384], replicated
- grad_embed_weight: float32 [768, 768], replicated
- grad_embed_offset: float32 [768], replicated
- grad_gain_second: float32 [384], replicated
- grad_shift_second: float32 [384], replicated
- grad_kernel_second: float32 [3, 3, 384, 384], replicated
- grad_offset_second: float32 [384], replicated
- grad_gain_attend: float32 [384], replicated
- grad_shift_attend: float32 [384], replicated
- grad_project_in: float32 [384, 1152], replicated
- grad_offset_in: float32 [768], replicated
- grad_project_out: float32 [384, 384], replicated
- grad_offset_out: float32 [384], replicated
Inputs may be any that keep to these rules, and one draw needn't show every extreme that they name: extents[i] = (valid rows, valid columns) of image i. Every image has more than 17 valid rows, and at least one image is valid at every pixel.
All inputs are finite; a program needn't handle non-finite values.
Results may differ from a plain program's by a relative error of at most 0.014.
Values may be sent and summed in bfloat16 or wider, within the bound.
A program may use at most 128 MiB of HBM per device.

v0:
```python
import math

import jax
import jax.numpy as jnp
from jax import lax
from jax.sharding import PartitionSpec as P

HEAD_DIM = 64
GROUPS = 32


PRECISE = lax.Precision.HIGHEST
EPSILON = 1e-05
MASKED = -1e30


def padded_2(shard, sides, width):
    for axis, dim in sides:
        size, length = (lax.axis_size(axis), shard.shape[dim])
        up = [(i, (i + 1) % size) for i in range(size - 1)]
        down = [(j, i) for i, j in up]
        last = lax.slice_in_dim(shard, length - width, length, axis=dim)
        initial = lax.slice_in_dim(shard, 0, width, axis=dim)
        before = lax.ppermute(last, axis, up)
        after = lax.ppermute(initial, axis, down)
        shard = jnp.concatenate([before, shard, after], axis=dim)
    return shard


def time_features(timesteps, width):
    half_width = width // 2
    frequency = jnp.exp(-math.log(10000.0) * jnp.arange(half_width, dtype=jnp.float32) / half_width)
    angles = timesteps.astype(jnp.float32)[:, None] * frequency[None, :]
    return jnp.concatenate([jnp.cos(angles), jnp.sin(angles)], axis=1)


def stripe_mask(extents, stripe_rows, columns):
    first_row = lax.axis_index("pix") * stripe_rows
    row_ids = first_row + jnp.arange(stripe_rows, dtype=jnp.int32)
    col_ids = jnp.arange(columns, dtype=jnp.int32)
    row_ok = row_ids[None, :] < extents[:, 0:1]
    col_ok = col_ids[None, :] < extents[:, 1:2]
    return (row_ok[:, :, None] & col_ok[:, None, :]).astype(jnp.float32)


def grouped_view(field):
    batch, stripe_rows, columns, channels = field.shape
    return field.reshape(batch, stripe_rows, columns, GROUPS, channels // GROUPS)


def apply_stats(field, group_mean, inv_std):
    grouped = grouped_view(field)
    normed = (grouped - group_mean[:, None, None, :, None]) * inv_std[:, None, None, :, None]
    return normed.reshape(field.shape)


def normalize(field, pixel_mask, entries):
    grouped = grouped_view(field)
    weight = pixel_mask[:, :, :, None, None]
    sum_part = jnp.sum(grouped * weight, axis=(1, 2, 4))
    square_part = jnp.sum(grouped * grouped * weight, axis=(1, 2, 4))
    totals, squares = lax.psum((sum_part, square_part), "pix")
    group_mean = totals / entries[:, None]
    inv_std = lax.rsqrt(squares / entries[:, None] - group_mean * group_mean + EPSILON)
    return (apply_stats(field, group_mean, inv_std), group_mean, inv_std)


def norm_back(dnormed, normed, inv_std, pixel_mask, entries):
    grad_view = grouped_view(dnormed)
    norm_view = grouped_view(normed)
    grad_total = jnp.sum(grad_view, axis=(1, 2, 4))
    grad_dot = jnp.sum(grad_view * norm_view, axis=(1, 2, 4))
    grad_total, grad_dot = lax.psum((grad_total, grad_dot), "pix")
    weight = pixel_mask[:, :, :, None, None]
    spread = (
        grad_total[:, None, None, :, None] + norm_view * grad_dot[:, None, None, :, None]
    ) / entries[:, None, None, None, None]
    return (inv_std[:, None, None, :, None] * (grad_view - weight * spread)).reshape(normed.shape)


def widen(acts):
    return padded_2(acts, (("pix", 1),), 1)


def convolve(wide, kernel):
    return lax.conv_general_dilated(
        wide,
        kernel,
        (1, 1),
        ((0, 0), (1, 1)),
        dimension_numbers=("NHWC", "HWIO", "NHWC"),
        preferred_element_type=jnp.float32,
    )


def convolve_back(dout, kernel):
    wide = padded_2(dout, (("pix", 1),), 1)
    flipped = jnp.transpose(kernel[::-1, ::-1], (0, 1, 3, 2))
    return convolve(wide, flipped)


def kernel_grad(wide, dout):
    batch, stripe_rows, columns, channels = dout.shape
    padded = jnp.pad(wide, ((0, 0), (0, 0), (1, 1), (0, 0)))
    flat_grad = dout.reshape(-1, channels)
    kernels = []
    for row_tap in range(3):
        for col_tap in range(3):
            window = padded[
                :, row_tap : row_tap + stripe_rows, col_tap : col_tap + columns, :
            ].reshape(-1, channels)
            kernels.append(
                lax.dot_general(
                    window, flat_grad, (((0,), (0,)), ((), ())), preferred_element_type=jnp.float32
                )
            )
    return jnp.stack(kernels).reshape(3, 3, channels, channels)


def bias_layout(offset_in, heads_all):
    pairs = offset_in.reshape(heads_all, 2, HEAD_DIM)
    key_zeros = jnp.zeros((heads_all, 1, HEAD_DIM), jnp.float32)
    return jnp.concatenate([pairs[:, 0:1], key_zeros, pairs[:, 1:2]], axis=1).reshape(
        3 * heads_all * HEAD_DIM
    )


def split_heads(heads_qkv):
    batch, length, width = heads_qkv.shape
    local_heads = width // (3 * HEAD_DIM)
    split_qkv = heads_qkv.reshape(batch, length, local_heads, 3, HEAD_DIM)
    return (split_qkv[:, :, :, 0], split_qkv[:, :, :, 1], split_qkv[:, :, :, 2])


def score_block(queries, key_vecs, key_flags):
    raw_scores = jnp.einsum(
        "bqhd,bkhd->bhqk", queries, key_vecs, preferred_element_type=jnp.float32
    ) / math.sqrt(HEAD_DIM)
    return jnp.where(key_flags[:, None, None, :, 0] > 0, raw_scores, MASKED)


def attend(heads_qkv, key_flags):
    batch, length, width = heads_qkv.shape
    queries, key_vecs, values = split_heads(heads_qkv)
    scores = score_block(queries, key_vecs, key_flags)
    maxima = jnp.max(scores, axis=-1, keepdims=True)
    shifted_exp = jnp.exp(scores - maxima)
    totals = jnp.sum(shifted_exp, axis=-1, keepdims=True)
    probabilities = (shifted_exp / totals).astype(jnp.bfloat16)
    attended = jnp.einsum(
        "bhqk,bkhd->bqhd", probabilities, values, preferred_element_type=jnp.float32
    )
    return (attended.astype(jnp.bfloat16).reshape(batch, length, width // 3), maxima, totals)


def attend_back(heads_qkv, key_flags, maxima, totals, d_attended):
    batch, length, width = heads_qkv.shape
    queries, key_vecs, values = split_heads(heads_qkv)
    scores = score_block(queries, key_vecs, key_flags)
    probabilities = jnp.exp(scores - maxima) / totals
    probs_low = probabilities.astype(jnp.bfloat16)
    grad_heads = d_attended.reshape(batch, length, width // (3 * HEAD_DIM), HEAD_DIM)
    d_probs = jnp.einsum("bqhd,bkhd->bhqk", grad_heads, values, preferred_element_type=jnp.float32)
    d_values = jnp.einsum(
        "bhqk,bqhd->bkhd", probs_low, grad_heads, preferred_element_type=jnp.float32
    )
    inner = jnp.sum(probabilities * d_probs, axis=-1, keepdims=True)
    d_scores = (probabilities * (d_probs - inner)).astype(jnp.bfloat16)
    d_queries = jnp.einsum(
        "bhqk,bkhd->bqhd", d_scores, key_vecs, preferred_element_type=jnp.float32
    ) / math.sqrt(HEAD_DIM)
    d_keys = jnp.einsum(
        "bhqk,bqhd->bkhd", d_scores, queries, preferred_element_type=jnp.float32
    ) / math.sqrt(HEAD_DIM)
    stacked = jnp.stack([d_queries, d_keys, d_values], axis=3)
    return stacked.astype(jnp.bfloat16).reshape(batch, length, width)


def silu_grad(pre, upstream):
    return jax.vjp(jax.nn.silu, pre)[1](upstream)[0]


def local(
    images_in,
    extents,
    timesteps,
    gain_first,
    shift_first,
    kernel_first,
    offset_first,
    embed_weight,
    embed_offset,
    gain_second,
    shift_second,
    kernel_second,
    offset_second,
    gain_attend,
    shift_attend,
    project_in,
    offset_in,
    project_out,
    offset_out,
    out_grad,
):
    batch, stripe_rows, columns, channels = images_in.shape
    heads_all = channels // HEAD_DIM
    pixels = stripe_rows * columns
    pixel_mask = stripe_mask(extents, stripe_rows, columns)
    entries = (extents[:, 0] * extents[:, 1]).astype(jnp.float32) * (channels // GROUPS)
    field_in = images_in.astype(jnp.float32)
    time_act = jax.nn.silu(time_features(timesteps, embed_weight.shape[0]))
    film = jnp.dot(time_act, embed_weight.astype(jnp.float32), precision=PRECISE) + embed_offset
    film_scale = film[:, None, None, :channels]
    film_shift = film[:, None, None, channels:]
    normed_one, mean_one, inv_one = normalize(field_in, pixel_mask, entries)
    pre_one = normed_one * gain_first + shift_first
    act_one = jax.nn.silu(pre_one).astype(jnp.bfloat16)
    wide_one = widen(act_one)
    conv_one = convolve(wide_one, kernel_first) + offset_first
    normed_two, mean_two, inv_two = normalize(conv_one, pixel_mask, entries)
    pre_two = (normed_two * gain_second + shift_second) * (1.0 + film_scale) + film_shift
    act_two = jax.nn.silu(pre_two).astype(jnp.bfloat16)
    wide_two = widen(act_two)
    hidden = field_in + (convolve(wide_two, kernel_second) + offset_second)
    normed_att, mean_att, inv_att = normalize(hidden, pixel_mask, entries)
    att_in = (normed_att * gain_attend + shift_attend).astype(jnp.bfloat16)
    flat_in = att_in.reshape(batch * pixels, channels)
    qkv = jnp.dot(flat_in, project_in, preferred_element_type=jnp.float32) + bias_layout(
        offset_in, heads_all
    )
    qkv = qkv.astype(jnp.bfloat16).reshape(batch, pixels, 3 * channels)
    flags = jnp.broadcast_to(
        pixel_mask.reshape(batch, pixels, 1).astype(jnp.int32),
        (batch, pixels, lax.axis_size("pix")),
    )
    heads_qkv, key_flags = (
        lax.all_to_all(qkv, "pix", split_axis=2, concat_axis=1, tiled=True),
        lax.all_to_all(flags, "pix", split_axis=2, concat_axis=1, tiled=True),
    )
    attended_heads, maxima, totals = attend(heads_qkv, key_flags)
    attended = lax.all_to_all(attended_heads, "pix", split_axis=1, concat_axis=2, tiled=True)
    att_flat = attended.reshape(batch * pixels, channels)
    projected = jnp.dot(att_flat, project_out, preferred_element_type=jnp.float32) + offset_out
    result = (hidden + projected.reshape(hidden.shape)).astype(jnp.bfloat16)
    grad_flat = out_grad.reshape(batch * pixels, channels)
    grad_field = out_grad.astype(jnp.float32)
    grad_project_out = lax.dot_general(
        att_flat, grad_flat, (((0,), (0,)), ((), ())), preferred_element_type=jnp.float32
    )
    grad_offset_out = jnp.sum(grad_field, axis=(0, 1, 2))
    d_attended = lax.dot_general(
        grad_flat, project_out, (((1,), (1,)), ((), ())), preferred_element_type=jnp.float32
    )
    d_attended = d_attended.astype(jnp.bfloat16).reshape(batch, pixels, channels)
    d_att_heads = lax.all_to_all(d_attended, "pix", split_axis=2, concat_axis=1, tiled=True)
    d_qkv_heads = attend_back(heads_qkv, key_flags, maxima, totals, d_att_heads)
    d_qkv = lax.all_to_all(d_qkv_heads, "pix", split_axis=1, concat_axis=2, tiled=True).reshape(
        batch * pixels, 3 * channels
    )
    grad_project_in = lax.dot_general(
        flat_in, d_qkv, (((0,), (0,)), ((), ())), preferred_element_type=jnp.float32
    )
    bias_sums = jnp.sum(d_qkv.astype(jnp.float32), axis=0).reshape(heads_all, 3, HEAD_DIM)
    grad_offset_in = jnp.concatenate([bias_sums[:, 0:1], bias_sums[:, 2:3]], axis=1).reshape(
        2 * channels
    )
    d_att_in = lax.dot_general(
        d_qkv, project_in, (((1,), (1,)), ((), ())), preferred_element_type=jnp.float32
    )
    d_att_in = d_att_in.reshape(hidden.shape)
    grad_gain_attend = jnp.sum(d_att_in * normed_att, axis=(0, 1, 2))
    grad_shift_attend = jnp.sum(d_att_in, axis=(0, 1, 2))
    d_hidden = grad_field + norm_back(
        d_att_in * gain_attend, normed_att, inv_att, pixel_mask, entries
    )
    saved = lax.optimization_barrier((field_in, mean_one, inv_one, mean_two, inv_two, d_hidden))
    field_again, mean_again, inv_again, mean_later, inv_later, d_hidden = saved
    normed_one = apply_stats(field_again, mean_again, inv_again)
    pre_one = normed_one * gain_first + shift_first
    act_one = jax.nn.silu(pre_one).astype(jnp.bfloat16)
    wide_one = widen(act_one)
    conv_one = convolve(wide_one, kernel_first) + offset_first
    normed_two = apply_stats(conv_one, mean_later, inv_later)
    pre_two = (normed_two * gain_second + shift_second) * (1.0 + film_scale) + film_shift
    act_two = jax.nn.silu(pre_two).astype(jnp.bfloat16)
    wide_two = widen(act_two)
    d_conv_two = d_hidden.astype(jnp.bfloat16)
    d_act_two = convolve_back(d_conv_two, kernel_second)
    d_pre_two = silu_grad(pre_two, d_act_two)
    affine_two = normed_two * gain_second + shift_second
    d_film = jnp.concatenate(
        [jnp.sum(d_pre_two * affine_two, axis=(1, 2)), jnp.sum(d_pre_two, axis=(1, 2))], axis=1
    )
    grad_embed_weight = lax.dot_general(
        time_act, d_film, (((0,), (0,)), ((), ())), precision=PRECISE
    )
    grad_embed_offset = jnp.sum(d_film, axis=0)
    d_affine_two = d_pre_two * (1.0 + film_scale)
    grad_gain_second = jnp.sum(d_affine_two * normed_two, axis=(0, 1, 2))
    grad_shift_second = jnp.sum(d_affine_two, axis=(0, 1, 2))
    d_conv_one = norm_back(
        d_affine_two * gain_second, normed_two, inv_two, pixel_mask, entries
    ).astype(jnp.bfloat16)
    d_act_one = convolve_back(d_conv_one, kernel_first)
    d_pre_one = silu_grad(pre_one, d_act_one)
    grad_gain_first = jnp.sum(d_pre_one * normed_one, axis=(0, 1, 2))
    grad_shift_first = jnp.sum(d_pre_one, axis=(0, 1, 2))
    in_grad = (
        d_hidden + norm_back(d_pre_one * gain_first, normed_one, inv_one, pixel_mask, entries)
    ).astype(jnp.bfloat16)
    grad_kernel_first = kernel_grad(wide_one, d_conv_one)
    grad_kernel_second = kernel_grad(wide_two, d_conv_two)
    grad_offset_first = jnp.sum(d_conv_one.astype(jnp.float32), axis=(0, 1, 2))
    grad_offset_second = jnp.sum(d_conv_two.astype(jnp.float32), axis=(0, 1, 2))
    summed = lax.psum(
        (
            grad_gain_first,
            grad_shift_first,
            grad_kernel_first,
            grad_offset_first,
            grad_embed_weight,
            grad_embed_offset,
            grad_gain_second,
            grad_shift_second,
            grad_kernel_second,
            grad_offset_second,
            grad_gain_attend,
            grad_shift_attend,
            grad_project_in,
            grad_offset_in,
            grad_project_out,
            grad_offset_out,
        ),
        ("img", "pix"),
    )
    return (
        result,
        in_grad,
        summed[0],
        summed[1],
        summed[2],
        summed[3],
        summed[4],
        summed[5],
        summed[6],
        summed[7],
        summed[8],
        summed[9],
        summed[10],
        summed[11],
        summed[12],
        summed[13],
        summed[14],
        summed[15],
    )


def solution(mesh):
    in_specs = (
        P("img", "pix", None, None),
        P("img", None),
        P("img"),
        P(),
        P(),
        P(),
        P(),
        P(),
        P(),
        P(),
        P(),
        P(),
        P(),
        P(),
        P(),
        P(),
        P(),
        P(),
        P(),
        P("img", "pix", None, None),
    )
    out_specs = (
        P("img", "pix", None, None),
        P("img", "pix", None, None),
        P(),
        P(),
        P(),
        P(),
        P(),
        P(),
        P(),
        P(),
        P(),
        P(),
        P(),
        P(),
        P(),
        P(),
        P(),
        P(),
    )
    return jax.shard_map(local, mesh=mesh, in_specs=in_specs, out_specs=out_specs, check_vma=False)
```

profile of v0, /device:TPU:0, one launch (start us, length us, event | category | flops | bytes accessed | tf_op | source)
XLA Modules:
  0.0 605.3 jit_solution(11620216930101601253)
XLA Ops:
  40.2 4.2 all-to-all-start.3
  73.9 3.8 collective-permute-start.2
  93.2 6.2 %copy.337 = bf16[1,512,1152]{1,0,2:T(2,128)(2,1)} copy(bf16[1,512,1152]{2,1,0:T(8,128)(2,1)} %fusion.10) | data formatting | bytes 2359296 | tf_op jit(solution)/shard_map/reshape | solution.py:231
  99.4 9.7 %reduce.66 = bf16[1152,512]{1,0:T(8,128)(2,1)} reduce(bf16[1152,1,512]{2,1,0:T(2,128)(2,1)} %bitcast.392, bf16[]{:T(256)} %broadcast.680), dimensions={1}, to_apply=%bitcast.337.reduce_sub_computation | reduce | bytes 2359298
  111.9 6.9 %all_to_all.69 = bf16[2,2,147456]{2,1,0:T(2,128)(2,1)} all-to-all(bf16[2,2,147456]{2,1,0:T(2,128)(2,1)} %reshape.969), channel_id=1, replica_groups=mesh['img'=16,'pix'=2] {'pix'}, dimensions={0} | all-to-all | bytes 2359296 | tf_op jit(solution)/shard_map/all_to_all | solution.py:237
  126.1 4.0 reshape.796
  130.0 10.0 %fusion.201 = (f32[3,1024]{1,0:T(4,128)S(1)}, f32[3,1024,1024]{1,2,0:T(8,128)}) fusion(pred[1024]{0:T(1024)(128)(4,1)S(1)} %copy-done.68, bf16[1,1024,3,3,64]{1,4,3,2,0:T(8,128)(2,1)} %reshape.796), kind=kOutput, calls=%fused_computation.308 | convolution fusion | flops 415237120 | bytes 13382656 | tf_op jit(solution)/shard_map/sub | solution.py:147
  140.1 6.9 %fusion.50 = bf16[1,1024,3,1,64]{1,4,2,3,0:T(8,128)(2,1)S(1)} fusion(bf16[1024,3,64]{0,2,1:T(8,128)(2,1)} %reshape.805, f32[3,1024,1024]{1,2,0:T(8,128)} %get-tuple-element.120, f32[3,1024]{1,0:T(4,128)S(1)} %get-tuple-element.119), kind=kOutput, calls=%fused_computation.83 | convolution fusion | flops 409141248 | bytes 13381632 | tf_op jit(solution)/shard_map/bhqk,bqhd->bkhd/dot_general | solution.py:164
  148.7 5.6 multiply_reduce_fusion
  154.3 7.1 %multiply_convert_fusion = bf16[3,1024,1024]{1,2,0:T(8,128)(2,1)S(1)} fusion(f32[3,1024,1024]{1,2,0:T(8,128)} %get-tuple-element.122, f32[3,1024]{1,0:T(4,128)S(1)} %get-tuple-element.121, f32[3,1024,1024]{1,2,0:T(8,128)S(1)} %copy-done.1, f32[3,1024]{1,0:T(4,128)S(1)} %get-tuple-element.119), kind=kLoop, calls=%fused_computation.1 | loop fusion | flops 12582912 | bytes 31481856 | tf_op jit(solution)/shard_map/convert_element_type | solution.py:168
  167.9 6.2 %copy.352 = bf16[1,1024,576]{2,0,1:T(2,128)(2,1)} copy(bf16[1,1024,576]{1,2,0:T(8,128)(2,1)} %bitcast.398) | data formatting | bytes 2359296 | tf_op jit(solution)/shard_map/convert_element_type | solution.py:176
  174.1 11.0 %reduce.67 = bf16[1024,576]{1,0:T(8,128)(2,1)} reduce(bf16[1024,1,576]{2,1,0:T(2,128)(2,1)} %bitcast.390, bf16[]{:T(256)} %broadcast.680), dimensions={1}, to_apply=%bitcast.343.reduce_sub_computation | reduce | bytes 2359298
  188.7 6.7 %all_to_all.70 = bf16[2,2,147456]{2,1,0:T(2,128)(2,1)} all-to-all(bf16[2,2,147456]{2,1,0:T(2,128)(2,1)} %reshape.975), channel_id=1, replica_groups=mesh['img'=16,'pix'=2] {'pix'}, dimensions={0} | all-to-all | bytes 2359296 | tf_op jit(solution)/shard_map/all_to_all | solution.py:257
  195.3 4.1 reshape.976
  202.4 3.9 copy.385
  207.9 3.8 multiply_reduce_fusion.8
  220.4 5.7 reduce.68
  228.4 5.9 all_to_all.71
  251.8 4.2 collective-permute-start.6
  269.8 5.1 select_reduce_fusion.1
  295.9 4.0 collective-permute-start.10
  338.9 44.1 %all-reduce.2 = (f32[384]{0:T(512)}, f32[384]{0:T(512)}, f32[384]{0:T(512)}, f32[768]{0:T(1024)}, f32[384]{0:T(512)}, /*index=5*/f32[384]{0:T(512)}, f32[384]{0:...) all-reduce(f32[384]{0:T(512)S(1)} %get-tuple-element.32, ...), channel_id=1, replica_groups=mesh['img'=16,'pix'=2] {'img','pix'}, use_global_device_ids=true, to_apply=%region_40.41 | all-reduce | flops 4992 | bytes 39936 | tf_op jit(solution)/shard_map/psum | solution.py:315
  385.5 200.4 %all-reduce.12.cloned.1.call-done = (f32[3,3,384,384]{3,2,1,0:T(8,128)}, f32[768,768]{1,0:T(8,128)}, f32[3,3,384,384]{3,2,1,0:T(8,128)}, f32[384,1152]{1,0:T(8,128)}, f32[384,384]{1,0:T(8,128)}) async-done(((f32[3,3,384,384]{3,2,1,0:T(8,128)}, f32[768,768]{1,0:T(8,128)}, f32[3,3,384,384]{3,2,1,0:T(8,128)}, f32[384,1152]{1,0:T(8,128)}, f32[384,384]{1,0:T(8,128)}), (f32[3,3,384,384]{3,2,1,0:T(8,128)}, ...) | async-done | bytes 15335440 | tf_op jit(solution)/shard_map/psum | solution.py:315
  585.9 5.7 copy.455
  (408 shorter events, 212.2 us)
Async XLA Ops:
  7.2 50.6 %copy-start = (bf16[3,3,384,384]{3,2,1,0:T(8,128)(2,1)S(1)}, bf16[3,3,384,384]{3,2,1,0:T(8,128)(2,1)}, u32[]{:S(2)}) copy-start(bf16[3,3,384,384]{3,2,1,0:T(8,128)(2,1)} %param.25) | copy-start | bytes 7962628
  7.2 22.0 %copy-start.57 = (f32[768]{0:T(1024)S(1)}, f32[768]{0:T(1024)}, u32[]{:S(2)}) copy-start(f32[768]{0:T(1024)} %param.28) | copy-start | bytes 9220
  7.2 22.1 %copy-start.6 = (bf16[1,16,32,384]{3,2,1,0:T(8,128)(2,1)S(1)}, bf16[1,16,32,384]{3,2,1,0:T(8,128)(2,1)}, u32[]{:S(2)}) copy-start(bf16[1,16,32,384]{3,2,1,0:T(8,128)(2,1)} %param.39) | copy-start | bytes 1179652
  15.8 22.1 %copy-start.36 = (f32[384]{0:T(512)}, f32[384]{0:T(512)S(1)}, u32[]{:S(2)}) copy-start(f32[384]{0:T(512)S(1)} %mul.582) | copy-start | bytes 4612
  18.2 38.1 %collective-permute-start.1 = (bf16[1,1,32,384]{3,2,1,0:T(8,128)(2,1)}, bf16[1,1,32,384]{3,2,1,0:T(8,128)(2,1)S(1)}, u32[]{:S(2)}, u32[]{:S(2)}) collective-permute-start(bf16[1,1,32,384]{3,2,1,0:T(8,128)(2,1)} %get-tuple-element.110), channel_id=1, source_target_pairs={{1,0},{3,2},{5,4},{7,6},{9,8},{11,10},{13,12},{15,14},{17,16},{19,... | collective-permute-start | bytes 73736 | tf_op jit(solution)/shard_map/ppermute | solution.py:25
  19.5 36.9 %collective-permute-start = (bf16[1,1,32,384]{3,2,1,0:T(8,128)(2,1)S(1)}, bf16[1,1,32,384]{3,2,1,0:T(8,128)(2,1)S(1)}, u32[]{:S(2)}, u32[]{:S(2)}) collective-permute-start(bf16[1,1,32,384]{3,2,1,0:T(8,128)(2,1)S(1)} %get-tuple-element.109), channel_id=1, source_target_pairs={{0,1},{2,3},{4,5},{6,7},{8,9},{10,11},{12,13},{14,15},{16,17},{18,... | collective-permute-start | bytes 73736 | tf_op jit(solution)/shard_map/ppermute | solution.py:24
  23.4 16.8 %all-to-all-start.1 = ((s32[1,512,2]{1,0,2:T(1,128)}), s32[1,512,2]{1,0,2:T(1,128)S(1)}, u32[]{:S(2)}, u32[]{:S(2)}) async-start(s32[1,512,2]{1,0,2:T(1,128)} %broadcast_in_dim.17), calls=%async_computation.1 | async-start | bytes 8192 | tf_op jit(solution)/shard_map/all_to_all | solution.py:238
  27.3 12.6 %copy-start.58 = (f32[768]{0:T(1024)S(1)}, f32[768]{0:T(1024)}, u32[]{:S(2)}) copy-start(f32[768]{0:T(1024)} %param.36) | copy-start | bytes 9220
  40.2 6.6 %all-to-all-start.3 = ((bf16[2,2,49152]{2,1,0:T(2,128)(2,1)}), bf16[2,2,49152]{2,1,0:T(2,128)(2,1)}, u32[]{:S(2)}, u32[]{:S(2)}) async-start(bf16[2,2,49152]{2,1,0:T(2,128)(2,1)} %reshape.973), calls=%async_computation.3 | async-start | bytes 786432 | tf_op jit(solution)/shard_map/all_to_all | solution.py:255
  44.3 541.5 %all-reduce.12.cloned.1.call-start = ((), (), s32[]{:S(2)}) async-start(), calls=%async_computation.5 | async-start | bytes 30670848 | tf_op jit(solution)/shard_map/psum | solution.py:315
  70.3 8.5 %collective-permute-start.3 = (bf16[1,1,32,384]{3,1,2,0:T(2,128)(2,1)}, bf16[1,1,32,384]{3,1,2,0:T(2,128)(2,1)}, u32[]{:S(2)}, u32[]{:S(2)}) collective-permute-start(bf16[1,1,32,384]{3,1,2,0:T(2,128)(2,1)} %slice.205), channel_id=1, source_target_pairs={{1,0},{3,2},{5,4},{7,6},{9,8},{11,10},{13,12},{15,14},{17,16},{19,... | collective-permute-start | bytes 73736 | tf_op jit(solution)/shard_map/ppermute | solution.py:25
  73.9 4.9 collective-permute-start.2
  247.1 12.3 %copy-start.54 = (f32[1,32]{1,0:T(1,128)S(1)}, f32[1,32]{1,0:T(1,128)}, u32[]{:S(2)}) copy-start(f32[1,32]{1,0:T(1,128)} %copy-done.53) | copy-start | bytes 388
  249.3 17.1 %copy-start.30 = (f32[384]{0:T(512)}, f32[384]{0:T(512)S(1)}, u32[]{:S(2)}) copy-start(f32[384]{0:T(512)S(1)} %mul.634) | copy-start | bytes 4612
  249.6 16.9 %copy-start.32 = (f32[384]{0:T(512)}, f32[384]{0:T(512)S(1)}, u32[]{:S(2)}) copy-start(f32[384]{0:T(512)S(1)} %sub.208) | copy-start | bytes 4612
  250.5 13.8 %collective-permute-start.7 = (bf16[1,1,32,384]{3,2,1,0:T(8,128)(2,1)}, bf16[1,1,32,384]{3,2,1,0:T(8,128)(2,1)}, u32[]{:S(2)}, u32[]{:S(2)}) collective-permute-start(bf16[1,1,32,384]{3,2,1,0:T(8,128)(2,1)} %get-tuple-element.108), channel_id=1, source_target_pairs={{1,0},{3,2},{5,4},{7,6},{9,8},{11,10},{13,12},{15,14},{17,16},{19,... | collective-permute-start | bytes 73736 | tf_op jit(solution)/shard_map/ppermute | solution.py:25
  251.8 12.5 %collective-permute-start.6 = (bf16[1,1,32,384]{3,2,1,0:T(8,128)(2,1)}, bf16[1,1,32,384]{3,2,1,0:T(8,128)(2,1)}, u32[]{:S(2)}, u32[]{:S(2)}) collective-permute-start(bf16[1,1,32,384]{3,2,1,0:T(8,128)(2,1)} %get-tuple-element.107), channel_id=1, source_target_pairs={{0,1},{2,3},{4,5},{6,7},{8,9},{10,11},{12,13},{14,15},{16,17},{18,... | collective-permute-start | bytes 73736 | tf_op jit(solution)/shard_map/ppermute | solution.py:24
  259.6 7.0 %collective-permute-start.5 = (bf16[1,1,32,384]{3,2,1,0:T(8,128)(2,1)}, bf16[1,1,32,384]{3,2,1,0:T(8,128)(2,1)S(1)}, u32[]{:S(2)}, u32[]{:S(2)}) collective-permute-start(bf16[1,1,32,384]{3,2,1,0:T(8,128)(2,1)} %get-tuple-element.106), channel_id=1, source_target_pairs={{1,0},{3,2},{5,4},{7,6},{9,8},{11,10},{13,12},{15,14},{17,16},{19,... | collective-permute-start | bytes 73736 | tf_op jit(solution)/shard_map/ppermute | solution.py:25
  260.9 5.7 collective-permute-start.4
  294.6 9.2 %collective-permute-start.11 = (bf16[1,1,32,384]{3,2,1,0:T(8,128)(2,1)}, bf16[1,1,32,384]{3,2,1,0:T(8,128)(2,1)}, u32[]{:S(2)}, u32[]{:S(2)}) collective-permute-start(bf16[1,1,32,384]{3,2,1,0:T(8,128)(2,1)} %slice.229), channel_id=1, source_target_pairs={{1,0},{3,2},{5,4},{7,6},{9,8},{11,10},{13,12},{15,14},{17,16},{19,... | collective-permute-start | bytes 73736 | tf_op jit(solution)/shard_map/ppermute | solution.py:25
  295.9 7.8 %collective-permute-start.10 = (bf16[1,1,32,384]{3,2,1,0:T(8,128)(2,1)S(1)}, bf16[1,1,32,384]{3,2,1,0:T(8,128)(2,1)S(1)}, u32[]{:S(2)}, u32[]{:S(2)}) collective-permute-start(bf16[1,1,32,384]{3,2,1,0:T(8,128)(2,1)S(1)} %slice.226), channel_id=1, source_target_pairs={{0,1},{2,3},{4,5},{6,7},{8,9},{10,11},{12,13},{14,15},{16,17},{18,... | collective-permute-start | bytes 73736 | tf_op jit(solution)/shard_map/ppermute | solution.py:24
  322.3 6.3 %collective-permute-start.9 = (bf16[1,1,32,384]{3,1,2,0:T(2,128)(2,1)}, bf16[1,1,32,384]{3,1,2,0:T(2,128)(2,1)S(1)}, u32[]{:S(2)}, u32[]{:S(2)}) collective-permute-start(bf16[1,1,32,384]{3,1,2,0:T(2,128)(2,1)} %get-tuple-element.104), channel_id=1, source_target_pairs={{1,0},{3,2},{5,4},{7,6},{9,8},{11,10},{13,12},{15,14},{17,16},{19,... | collective-permute-start | bytes 73736 | tf_op jit(solution)/shard_map/ppermute | solution.py:25
  323.6 5.0 collective-permute-start.8
  333.5 49.5 %copy-start.37 = (f32[384]{0:T(512)S(1)}, f32[384]{0:T(512)}, u32[]{:S(2)}) copy-start(f32[384]{0:T(512)} %copy-done.36) | copy-start | bytes 4612
  (68 other events, 301.5 us)
Sparse Core Ops, SparseCore 0:
  316.5 269.3 all-reduce.11
where the time goes:
time: 617 us; the launch traced here: 605 us
  waiting for transfers between devices  200 us (32%)
  local copies, waits for them, and re-layouts  116 us (19%)
  matrix products  84.3 us (14%)
  blocking collectives  78.7 us (13%)
  other arithmetic  71.2 us (12%)
  starting transfers between devices  36.5 us (6%)
  between operations  18 us (3%)
    psum x1, waiting for transfers between devices, local(): lax.psum((grad_gain_first, grad_shift_first, grad_kernel_first, grad_offs...  200 us
    unnamed x176, local copies, waits for them, and re-layouts  48.5 us
    psum x1, blocking collectives, local(): lax.psum((grad_gain_first, grad_shift_first, grad_kernel_first, grad_offs...  44.1 us
    unnamed x4, other arithmetic  30.1 us
    dot_general x18, matrix products, kernel_grad(): lax.dot_general(window, flat_grad, (((0,), (0,)), ((), ())), preferred_el...  24.5 us
    ppermute x6, starting transfers between devices, padded_2(): before = lax.ppermute(last, axis, up)  21.4 us
    conv_general_dilated x5, matrix products, convolve(): lax.conv_general_dilated(wide, kernel, (1, 1), ((0, 0), (1, 1)), dimensio...  15.8 us
  transfers between devices with their start and end apart: 15, of which 1 were waited for; matrix products, arithmetic and copies ran while one was open for 9% of the time, Pallas kernels for 0%

commit v1 on v0

v1 whole, which is shorter than its diff:
```python
import functools
import math

import jax
import jax.numpy as jnp
from jax import lax
from jax.experimental import pallas as pl
from jax.experimental.pallas import tpu as pltpu
from jax.sharding import PartitionSpec as P

HEAD_DIM = 64
GROUPS = 32
EPSILON = 1e-05
MASKED = -1e30
BF = jnp.bfloat16
F32 = jnp.float32
MESH = pl.DeviceIdType.MESH
WIN = 256
LANES = 128
RC = 128
MC = 256
QC = 256


def dot(a, b):
    return jnp.dot(a, b, preferred_element_type=F32)


def dot_nt(a, b):
    return lax.dot_general(a, b, (((1,), (1,)), ((), ())), preferred_element_type=F32)


def dot_hi(a, b):
    return jnp.dot(a, b, preferred_element_type=F32, precision=lax.Precision.HIGHEST)


def fold(v):
    return jnp.sum(v.reshape(v.shape[0] // 8, 8, v.shape[1]), axis=0)


def sigmoid(v):
    return 1.0 / (1.0 + jnp.exp(-v))


def cdiv(a, b):
    return -(-a // b)


class Flow:
    def __init__(self, pay, rbuf, out, base, rows, order, sems, core, img):
        self.pay, self.rbuf, self.out, self.lo, self.size = pay, rbuf, out, base, rows
        self.rbase = base
        self.order, self.sems, self.core, self.img = order, sems, core, img
        self.steps = len(order)
        self.k = -1
        self.cp = None
        self.fwd = []

    def peer(self, bit):
        mine = (self.img // bit) % 2
        return self.img + bit * (1 - 2 * mine), mine

    def sem(self, k):
        send, recv, first = self.sems
        return send.at[first + k], recv.at[first + k]

    def forward(self, lo, size, k):
        s, r = self.sem(k)
        ref = self.out.at[self.core, pl.ds(pl.multiple_of(lo, 16), size)]
        cp = pltpu.make_async_remote_copy(
            src_ref=ref, dst_ref=ref, send_sem=s, recv_sem=r, device_id=(self.img, 1 - self.core), device_id_type=MESH
        )
        cp.start()
        self.fwd.append(cp)

    def start(self):
        k = self.k
        n = self.steps
        s, r = self.sem(k)
        if k < n:
            peer, mine = self.peer(self.order[k])
            half = self.size // 2
            self.keep = pl.multiple_of(self.lo + mine * half, 16)
            send = pl.multiple_of(self.lo + (1 - mine) * half, 16)
            src = self.pay.at[pl.ds(send, half)]
            dst = self.rbuf.at[pl.ds(self.rbase, half)]
        else:
            peer, mine = self.peer(self.order[2 * n - 1 - k])
            self.mine = mine
            src = self.out.at[self.core, pl.ds(self.lo, self.size)]
            dst = src
        self.cp = pltpu.make_async_remote_copy(
            src_ref=src, dst_ref=dst, send_sem=s, recv_sem=r, device_id=(peer, self.core), device_id_type=MESH
        )
        self.cp.start()

    def finish(self):
        k, n = self.k, self.steps
        self.cp.wait()
        if k < n:
            half = self.size // 2
            keep, rbase = self.keep, self.rbase
            step = 16
            for cand in (512, 256, 128, 64, 32):
                if half % cand == 0:
                    step = cand
                    break

            def add(j, _):
                at = pl.ds(pl.multiple_of(keep + j * step, 16), step)
                rat = pl.ds(pl.multiple_of(rbase + j * step, 16), step)
                v = (self.pay[at, :].astype(F32) + self.rbuf[rat, :].astype(F32)).astype(BF)
                if k == n - 1:
                    self.out[self.core, at, :] = v
                else:
                    self.pay[at, :] = v
                return 0

            lax.fori_loop(0, half // step, add, 0)
            self.lo, self.size = keep, half
            self.rbase += half
        else:
            sib = self.lo + (1 - 2 * self.mine) * self.size
            if k == 2 * n - 1:
                self.forward(self.lo, self.size, 2 * n)
                self.forward(sib, self.size, 2 * n + 1)
            self.lo = pl.multiple_of(self.lo - self.mine * self.size, 16)
            self.size *= 2

    def advance(self):
        if self.k >= 2 * self.steps:
            return
        if self.k >= 0:
            self.finish()
        self.k += 1
        if self.k < 2 * self.steps:
            self.start()

    def wait_forward(self):
        for cp in self.fwd:
            cp.wait()


def block_kernel(dims, *refs):
    side, chans, n_img, real_k, real_p, bits = dims
    (
        x_in, g_in, ext, p_g1, p_s1, p_o1, p_g2, p_s2, p_o2, p_g3, p_s3, p_oo, t_act, e_off, off_in, k1_h, k2_h, wi_h, wo_h, ew_h,
        res_out, ing_out, pk1_o, pk2_o, pp_o, vec_o,
        k1, k2, wo, ew, wq, xw, gf, mask, film, act1, act2, act3, dd2, dd1,
        cv, hid, tmp, resid, qa, ka, va, kat, vat, dot_t, att_t, dk, dv, dqt, dqkv,
        tsum, trecv, datt_s, datt_r, dm, act_t, ing_r,
        pay1, pay2, payp, rb1, rb2, rbp, out1, out2, outp, vx, vr, vall,
        lsem, xs, xr, fs, fr,
    ) = refs
    img = lax.axis_index("img")
    c = lax.axis_index("pix")
    oc = 1 - c
    px = side * side
    half = px // 2
    own_chans = chans // 2
    heads = own_chans // HEAD_DIM
    first = c == 0
    nbits = len(bits)

    def aligned(v, m):
        return pl.multiple_of(v, m)

    def rows_at(j, size):
        return pl.ds(aligned(j * size, size), size)

    def pad_at(j, size, shift=side):
        return pl.ds(aligned(j * size + shift, 32), size)

    win = pl.ds(aligned(LANES * c, LANES), WIN)
    owin = pl.ds(aligned(LANES * oc, LANES), WIN)

    barrier = pltpu.get_barrier_semaphore()
    peers = [(img, oc)]
    for bit in bits:
        peers.append((img + bit * (1 - 2 * ((img // bit) % 2)), c))
    for peer in peers:
        pl.semaphore_signal(barrier, inc=1, device_id=peer, device_id_type=MESH)

    loads = []
    for k, (src, dst) in enumerate(((wi_h, dqkv.at[pl.ds(0, chans)]), (ew_h, ew), (wo_h, wo.at[pl.ds(0, chans)]), (k1_h, k1), (k2_h, k2))):
        cp = pltpu.make_async_copy(src, dst, lsem.at[k])
        cp.start()
        loads.append(cp)
    pl.semaphore_wait(barrier, len(peers))

    def swap(src, dst, k):
        cp = pltpu.make_async_remote_copy(
            src_ref=src, dst_ref=dst, send_sem=xs.at[k], recv_sem=xr.at[k], device_id=(img, oc), device_id_type=MESH
        )
        cp.start()
        return cp

    my_rows = pl.ds(aligned(half * c, half), half)
    other_rows = pl.ds(aligned(half * oc, half), half)
    swap_x = swap(x_in.at[:, owin], xw.at[my_rows], 0)
    swap_g = swap(g_in, gf.at[my_rows], 1)
    xw[my_rows, :] = x_in[:, win]
    gf[my_rows, :] = g_in[...]

    lane = lax.broadcasted_iota(jnp.int32, (1, WIN), 1)
    own_f = (jnp.where(first, lane, WIN - 1 - lane) < own_chans).astype(F32)
    rows_e = ext[0, 0]
    cols_e = ext[0, 1]
    per = chans // GROUPS
    inv_entries = 1.0 / jnp.full((1, WIN), rows_e * cols_e * per, jnp.int32).astype(F32)
    gi = lax.broadcasted_iota(jnp.int32, (WIN, WIN), 0) + LANES * c
    gj = lax.broadcasted_iota(jnp.int32, (WIN, WIN), 1) + LANES * c
    same = (gi // per == gj // per).astype(F32)

    def pvec(ref):
        return ref[win].reshape(1, WIN)

    gain1, shift1, offset1 = pvec(p_g1), pvec(p_s1), pvec(p_o1)
    gain2, shift2, offset2 = pvec(p_g2), pvec(p_s2), pvec(p_o2)
    gain3, shift3 = pvec(p_g3), pvec(p_s3)

    def group_totals(a, b):
        both = dot_hi(jnp.concatenate([a, b], axis=0), same)
        return jnp.sum(both[:8], axis=0, keepdims=True), jnp.sum(both[8:], axis=0, keepdims=True)

    def total(a):
        return jnp.sum(a, axis=0, keepdims=True)

    zero8 = jnp.zeros((8, WIN), F32)

    def fill_mask(j, _):
        p = lax.broadcasted_iota(jnp.int32, (RC, LANES), 0) + j * RC
        ok = (p // side < rows_e) & (p % side < cols_e)
        mask[rows_at(j, RC), :] = ok.astype(F32)
        return 0

    lax.fori_loop(0, px // RC, fill_mask, 0)

    def mask2(j, size=RC):
        m = mask[rows_at(j, size), :]
        return jnp.concatenate([m, m], axis=1)

    edge = jnp.zeros((side, WIN), BF)
    for buf in (act1, act2, dd2, dd1):
        for s in range(2):
            buf[s, pl.ds(0, side), :] = edge
            buf[s, pl.ds(side + px, side), :] = edge
    for b in range(3):
        dm[b, pl.ds(0, side), :] = edge
        dm[b, pl.ds(side + px, side), :] = edge
    for pay, real in ((pay1, real_k), (pay2, real_k), (payp, real_p)):
        rest = pay.shape[0] - real
        if rest:
            pay[pl.ds(real, rest), :] = jnp.zeros((rest, LANES), BF)
    wo[pl.ds(chans, WIN - own_chans), :] = jnp.zeros((WIN - own_chans, chans), BF)
    for h in range(heads):
        dot_t[h, pl.ds(HEAD_DIM, HEAD_DIM), :] = jnp.zeros((HEAD_DIM, px), BF)
    att_t[pl.ds(own_chans, WIN - own_chans), :] = jnp.zeros((WIN - own_chans, px), BF)
    vx[...] = jnp.zeros(vx.shape, F32)

    lane1 = lax.broadcasted_iota(jnp.int32, (1, LANES), 1)
    low1 = lane1 < HEAD_DIM
    loads[0].wait()
    for k in range(3 * heads):
        place = 3 * heads * c + k
        blk = dqkv[pl.ds(0, chans), pl.ds(aligned((place // 2) * LANES, LANES), LANES)].astype(F32)
        blk = jnp.where(place % 2 == 0, blk, pltpu.roll(blk, HEAD_DIM, 1))
        wq[:, pl.ds(k * LANES, LANES)] = jnp.where(low1, blk, 0.0).astype(BF)

    loads[1].wait()
    t = t_act[...]
    t_a = t.astype(BF).astype(F32)
    t_b = (t - t_a).astype(BF).astype(F32)
    row16 = lax.broadcasted_iota(jnp.int32, (16, t.shape[1]), 0)
    t_rows = jnp.where(row16 == 0, t_a, jnp.where(row16 == 1, t_b, jnp.where(row16 == 2, t - t_a - t_b, 0.0)))
    film[...] = total(dot(t_rows.astype(BF), ew[...])) + e_off[...].reshape(1, -1)
    scale2 = 1.0 + film[:, win]
    move2 = film[:, pl.ds(aligned(chans + LANES * c, LANES), WIN)]

    swap_x.wait()

    def stats_step(v, m, carry):
        vm = v * m
        return carry[0] + fold(vm), carry[1] + fold(vm * v)

    def moments(carry):
        s, q = group_totals(*carry)
        mean = s * inv_entries
        return mean, lax.rsqrt(q * inv_entries - mean * mean + EPSILON)

    def body(j, carry):
        return stats_step(xw[rows_at(j, RC), :].astype(F32), mask2(j), carry)

    mean1, rstd1 = moments(lax.fori_loop(0, px // RC, body, (zero8, zero8)))
    mul1 = rstd1 * gain1
    add1 = shift1 - mean1 * mul1

    def body(j, _):
        pre = xw[rows_at(j, RC), :].astype(F32) * mul1 + add1
        act1[c, pad_at(j, RC), :] = (pre * sigmoid(pre) * own_f).astype(BF)
        return 0

    lax.fori_loop(0, px // RC, body, 0)
    inner = pl.ds(side, px)
    swap_a1 = swap(act1.at[c, inner], act1.at[c, inner], 2)

    loads[2].wait()
    swap_g.wait()
    wo_rows = pl.ds(aligned(own_chans * c, HEAD_DIM), own_chans)

    def body(j, _):
        o = dot_nt(wo[wo_rows, :], gf[rows_at(j, QC), :])
        for h in range(heads):
            dot_t[h, pl.ds(0, HEAD_DIM), rows_at(j, QC)] = o[HEAD_DIM * h : HEAD_DIM * (h + 1)].astype(BF)
        return 0

    lax.fori_loop(0, px // QC, body, 0)

    col = lax.broadcasted_iota(jnp.int32, (MC, WIN), 0) % side
    not_first = (col != 0).astype(F32)
    not_last = (col != side - 1).astype(F32)

    def conv(acts, s, kern, back, j):
        accs = []
        for b in range(3):
            acc = None
            for a in range(3):
                lhs = acts[s, pl.ds(aligned(j * MC + side * a, 32), MC), :]
                if back:
                    tap = (2 - a) * 3 + 2 - b
                    rhs = kern[pl.ds(aligned(tap * chans + LANES * c, LANES), WIN), pl.ds(aligned(LANES * s, LANES), WIN)]
                    o = dot_nt(lhs, rhs)
                else:
                    tap = a * 3 + b
                    rhs = kern[pl.ds(aligned(tap * chans + LANES * s, LANES), WIN), win]
                    o = dot(lhs, rhs)
                acc = o if acc is None else acc + o
            accs.append(acc)
        return accs[1] + pltpu.roll(accs[0], 1, 0) * not_first + pltpu.roll(accs[2], MC - 1, 0) * not_last

    loads[3].wait()

    def body(j, _):
        cv[rows_at(j, MC), :] = conv(act1, c, k1, False, j)
        return 0

    lax.fori_loop(0, px // MC, body, 0)
    swap_a1.wait()

    def body(j, carry):
        v = cv[rows_at(j, MC), :] + conv(act1, oc, k1, False, j) + offset1
        cv[rows_at(j, MC), :] = v
        return stats_step(v, mask2(j, MC), carry)

    mean2, rstd2 = moments(lax.fori_loop(0, px // MC, body, (zero8, zero8)))
    mul2 = rstd2 * gain2 * scale2
    add2 = (shift2 - mean2 * rstd2 * gain2) * scale2 + move2

    def body(j, _):
        pre = cv[rows_at(j, RC), :] * mul2 + add2
        act2[c, pad_at(j, RC), :] = (pre * sigmoid(pre) * own_f).astype(BF)
        return 0

    lax.fori_loop(0, px // RC, body, 0)
    swap_a2 = swap(act2.at[c, inner], act2.at[c, inner], 3)

    loads[4].wait()

    def body(j, _):
        at = rows_at(j, MC)
        hid[at, :] = conv(act2, c, k2, False, j) + offset2 + xw[at, :].astype(F32)
        return 0

    lax.fori_loop(0, px // MC, body, 0)
    swap_a2.wait()

    def body(j, carry):
        v = hid[rows_at(j, MC), :] + conv(act2, oc, k2, False, j)
        hid[rows_at(j, MC), :] = v
        return stats_step(v, mask2(j, MC), carry)

    mean3, rstd3 = moments(lax.fori_loop(0, px // MC, body, (zero8, zero8)))
    mul3 = rstd3 * gain3
    add3 = shift3 - mean3 * mul3

    def body(j, _):
        act3[c, rows_at(j, RC), :] = ((hid[rows_at(j, RC), :] * mul3 + add3) * own_f).astype(BF)
        return 0

    lax.fori_loop(0, px // RC, body, 0)
    swap_a3 = swap(act3.at[c], act3.at[c], 4)

    biases = []
    for h in range(heads):
        blk = off_in[pl.ds(aligned(LANES * (heads * c + h), LANES), LANES)].reshape(1, LANES)
        turned = pltpu.roll(jnp.broadcast_to(blk, (8, LANES)), HEAD_DIM, 1)[:1]
        bias_q = jnp.where(low1, blk, jnp.where(lane1 == HEAD_DIM, 8.0, 0.0))
        bias_v = jnp.where(low1, turned, jnp.where(lane1 < HEAD_DIM + 2, 1.0, 0.0))
        biases.append((bias_q, bias_v))
    swap_a3.wait()

    def body(j, _):
        at = rows_at(j, MC)
        a0 = act3[0, at, :]
        a1 = act3[1, at, :]
        hidden_key = (mask[at, :] == 0.0) & (lane1 == HEAD_DIM)
        for h in range(heads):
            cols = pl.ds(3 * LANES * h, 3 * LANES)
            o = dot(a0, wq[pl.ds(0, WIN), cols]) + dot(a1, wq[pl.ds(LANES, WIN), cols])
            q = (o[:, :LANES] + biases[h][0]).astype(BF).astype(F32) * 0.125
            k = jnp.where(hidden_key, MASKED, o[:, LANES : 2 * LANES])
            v = o[:, 2 * LANES :] + biases[h][1]
            qa[h, at, :] = q.astype(BF)
            ka[h, at, :] = k.astype(BF)
            va[h, at, :] = v.astype(BF)
            kat[h, :, at] = k.T.astype(BF)
            vat[h, :, at] = v.T.astype(BF)
        return 0

    lax.fori_loop(0, px // MC, body, 0)

    dk[...] = jnp.zeros(dk.shape, F32)
    dv[...] = jnp.zeros(dv.shape, F32)
    row128 = lax.broadcasted_iota(jnp.int32, (LANES, QC), 0)

    def body(it, _):
        h = it // (px // QC)
        j = it % (px // QC)
        at = rows_at(j, QC)
        qc = qa[h, at, :]
        scores = dot_nt(ka[h], qc)
        top = jnp.max(scores, axis=0, keepdims=True)
        e = jnp.exp(scores - top).astype(BF)
        o = dot(vat[h], e)
        inv = 1.0 / o[HEAD_DIM : HEAD_DIM + 1, :]
        o = o * inv
        att_t[pl.ds(aligned(HEAD_DIM * h, HEAD_DIM), HEAD_DIM), at] = o[:HEAD_DIM].astype(BF)
        g = dot_t[h, :, at].astype(F32)
        less = -inv * jnp.sum(g * o, axis=0, keepdims=True)
        high = less.astype(BF).astype(F32)
        g = jnp.where(row128 == HEAD_DIM, high, jnp.where(row128 == HEAD_DIM + 1, less - high, g * inv)).astype(BF)
        ds = (e.astype(F32) * dot(va[h], g)).astype(BF)
        dv[h] += dot_nt(e, g)
        dk[h] += dot(ds, qc)
        dqt[h, :, at] = dot(kat[h], ds)
        return 0

    lax.fori_loop(0, heads * (px // QC), body, 0)

    for h in range(heads):

        def body(j, carry, h=h):
            at = rows_at(j, MC)
            parts = (dqt[h, :, at].T * 0.125, dk[h, at, :], dv[h, at, :])
            parts = [jnp.where(low1, p, 0.0).astype(BF) for p in parts]
            for k, p in enumerate(parts):
                dqkv[at, pl.ds((3 * h + k) * LANES, LANES)] = p
            return carry[0] + fold(parts[0].astype(F32)), carry[1] + fold(parts[2].astype(F32))

        z = jnp.zeros((8, LANES), F32)
        sum_q, sum_v = lax.fori_loop(0, px // MC, body, (z, z))
        sums = total(sum_q + pltpu.roll(sum_v, HEAD_DIM, 1))
        vx[pl.ds(13, 1), pl.ds(LANES * h, LANES)] = jnp.where(first, sums, 0.0)
        vx[pl.ds(14, 1), pl.ds(LANES * h, LANES)] = jnp.where(first, 0.0, sums)

    def body(j, _):
        at = rows_at(j, MC)
        datt_s[at, :] = dot_nt(dqkv[at, :], wq[owin, :]).astype(BF)
        return 0

    lax.fori_loop(0, px // MC, body, 0)
    swap_da = swap(datt_s, datt_r, 5)

    def body(j, _):
        at = rows_at(j, MC)
        tmp[at, :] = dot_nt(dqkv[at, :], wq[win, :])
        return 0

    lax.fori_loop(0, px // MC, body, 0)

    def turn(acts, shift):
        def body(j, _):
            a0 = acts[0, pad_at(j, MC, shift), :].astype(F32)
            a1 = acts[1, pad_at(j, MC, shift), :].astype(F32)
            at = rows_at(j, MC)
            act_t[pl.ds(0, LANES), at] = a0[:, :LANES].T.astype(BF)
            act_t[pl.ds(LANES, LANES), at] = (a0[:, LANES:] + a1[:, :LANES]).T.astype(BF)
            act_t[pl.ds(2 * LANES, LANES), at] = a1[:, LANES:].T.astype(BF)
            return 0

        lax.fori_loop(0, px // MC, body, 0)

    turn(act3, 0)
    for k in range(3 * heads // 2):
        o = dot(act_t[...], dqkv[:, pl.ds(2 * LANES * k, 2 * LANES)])
        pair = o[:, :LANES] + pltpu.roll(o[:, LANES:], HEAD_DIM, 1)
        payp[pl.ds(k * chans, chans), :] = pair.astype(BF)
    base = (3 * heads // 2) * chans
    if (3 * heads) % 2:
        o = dot(act_t[...], dqkv[:, pl.ds((3 * heads - 1) * LANES, LANES)])
        pair = o[: chans // 2] + pltpu.roll(o[chans // 2 :], HEAD_DIM, 1)
        payp[pl.ds(base, chans // 2), :] = pair.astype(BF)
        base += chans // 2
    o = dot(att_t[pl.ds(0, own_chans), :], gf[...])
    for b in range(chans // LANES):
        payp[pl.ds(base + b * own_chans, own_chans), :] = o[:, b * LANES : (b + 1) * LANES].astype(BF)

    used = [0]

    def flows(pay, rbuf, gathered):
        rows = pay.shape[0]
        units = rows // (16 * n_img)
        cut = (units // 2) * 16 * n_img
        swapped = [bits[1], bits[0]] + list(bits[2:])
        out = []
        for base, size, order in ((0, cut, list(bits)), (cut, rows - cut, swapped)):
            if size:
                out.append(Flow(pay, rbuf, gathered, base, size, order, (fs, fr, used[0]), c, img))
            used[0] += 2 * nbits + 2
        return out

    running = flows(payp, rbp, outp)

    def step():
        for flow in running:
            flow.advance()

    step()

    def body(j, _):
        at = rows_at(j, MC)
        tsum[at, :] = dot(att_t[:, at].astype(F32).T.astype(BF), wo[pl.ds(aligned(own_chans * c, HEAD_DIM), WIN), :])
        tsum[at, win] += hid[at, :] * own_f
        return 0

    lax.fori_loop(0, px // MC, body, 0)
    swap_t = swap(tsum.at[other_rows], trecv, 6)
    step()

    swap_da.wait()

    def back_sums(carry, u, normed):
        return carry[0] + fold(u), carry[1] + fold(u * normed)

    def body(j, carry):
        at = rows_at(j, RC)
        u = tmp[at, :] + datt_r[at, :].astype(F32)
        tmp[at, :] = u
        return back_sums(carry, u, (hid[at, :] - mean3) * rstd3)

    s0, s1 = lax.fori_loop(0, px // RC, body, (zero8, zero8))
    vx[pl.ds(6, 1), win] = total(s1) * own_f
    vx[pl.ds(7, 1), win] = total(s0) * own_f

    def spread_of(s0, s1, gain):
        a, b = group_totals(s0 * gain, s1 * gain)
        return a * inv_entries, b * inv_entries

    sp_a, sp_b = spread_of(s0, s1, gain3)

    def body(j, carry):
        at = rows_at(j, RC)
        normed = (hid[at, :] - mean3) * rstd3
        d = gf[at, win].astype(F32) + rstd3 * (tmp[at, :] * gain3 - mask2(j) * (sp_a + normed * sp_b))
        resid[at, :] = d
        low = (d * own_f).astype(BF)
        dd2[c, pad_at(j, RC), :] = low
        return carry + fold(low.astype(F32))

    vx[pl.ds(5, 1), win] = total(lax.fori_loop(0, px // RC, body, zero8))
    swap_d2 = swap(dd2.at[c, inner], dd2.at[c, inner], 7)
    step()

    def body(j, _):
        tmp[rows_at(j, MC), :] = conv(dd2, c, k2, True, j)
        return 0

    lax.fori_loop(0, px // MC, body, 0)
    step()
    turn(act2, side)
    swap_d2.wait()

    def kernel_grad(dd, pay):
        def body(j, _):
            d = dd[c, pad_at(j, MC), :].astype(F32)
            mid = dd[oc, pad_at(j, MC), pl.ds(aligned(LANES * c, LANES), LANES)].astype(F32)
            none = jnp.zeros((MC, LANES), F32)
            d = d + jnp.where(first, jnp.concatenate([none, mid], axis=1), jnp.concatenate([mid, none], axis=1))
            at = pad_at(j, MC)
            dm[0, at, :] = (pltpu.roll(d, MC - 1, 0) * not_last).astype(BF)
            dm[1, at, :] = d.astype(BF)
            dm[2, at, :] = (pltpu.roll(d, 1, 0) * not_first).astype(BF)
            return 0

        lax.fori_loop(0, px // MC, body, 0)
        hc = chans // 2

        def body(tap, _):
            a = tap // 3
            b = tap % 3
            o = dot(act_t[...], dm[b, pl.ds(aligned(side * (2 - a), 32), px), :])
            lo, hi = o[:, :LANES], o[:, LANES:]
            main = jnp.where(first, lo, hi)
            mid = jnp.where(first, hi[:hc], lo[hc:])
            pay[pl.ds(aligned(tap * chans, LANES), chans), :] = main.astype(BF)
            pay[pl.ds(aligned(9 * chans + tap * hc, HEAD_DIM), hc), :] = mid.astype(BF)
            return 0

        lax.fori_loop(0, 9, body, 0)

    kernel_grad(dd2, pay2)
    running.extend(flows(pay2, rb2, out2))
    step()

    def body(j, carry):
        at = rows_at(j, MC)
        pre = cv[at, :] * mul2 + add2
        sg = sigmoid(pre)
        u = (tmp[at, :] + conv(dd2, oc, k2, True, j)) * (sg * (1.0 + pre * (1.0 - sg)))
        tmp[at, :] = u
        return back_sums(carry, u, (cv[at, :] - mean2) * rstd2)

    s0, s1 = lax.fori_loop(0, px // MC, body, (zero8, zero8))
    t0, t1 = total(s0), total(s1)
    vx[pl.ds(9, 1), win] = (gain2 * t1 + shift2 * t0) * own_f
    vx[pl.ds(10, 1), win] = t0 * own_f
    vx[pl.ds(3, 1), win] = scale2 * t1 * own_f
    vx[pl.ds(4, 1), win] = scale2 * t0 * own_f
    gain2s = gain2 * scale2
    sp_a, sp_b = spread_of(s0, s1, gain2s)

    def body(j, carry):
        at = rows_at(j, RC)
        normed = (cv[at, :] - mean2) * rstd2
        d = rstd2 * (tmp[at, :] * gain2s - mask2(j) * (sp_a + normed * sp_b))
        low = (d * own_f).astype(BF)
        dd1[c, pad_at(j, RC), :] = low
        return carry + fold(low.astype(F32))

    vx[pl.ds(2, 1), win] = total(lax.fori_loop(0, px // RC, body, zero8))
    swap_d1 = swap(dd1.at[c, inner], dd1.at[c, inner], 8)
    step()

    def body(j, _):
        tmp[rows_at(j, MC), :] = conv(dd1, c, k1, True, j)
        return 0

    lax.fori_loop(0, px // MC, body, 0)
    step()
    turn(act1, side)
    swap_d1.wait()
    kernel_grad(dd1, pay1)
    running.extend(flows(pay1, rb1, out1))
    step()

    def body(j, carry):
        at = rows_at(j, MC)
        x = xw[at, :].astype(F32)
        pre = x * mul1 + add1
        sg = sigmoid(pre)
        u = (tmp[at, :] + conv(dd1, oc, k1, True, j)) * (sg * (1.0 + pre * (1.0 - sg)))
        tmp[at, :] = u
        return back_sums(carry, u, (x - mean1) * rstd1)

    s0, s1 = lax.fori_loop(0, px // MC, body, (zero8, zero8))
    vx[pl.ds(0, 1), win] = total(s1) * own_f
    vx[pl.ds(1, 1), win] = total(s0) * own_f
    step()

    g_sum = jnp.zeros((8, chans), F32)

    def body(j, carry):
        return carry + fold(gf[rows_at(j, RC), :].astype(F32))

    g_sum = total(lax.fori_loop(0, px // RC, body, g_sum))
    vx[pl.ds(8, 1), :] = jnp.where(first, g_sum, 0.0)
    for k in range(2):
        vx[pl.ds(11 + k, 1), :] = jnp.where(first, t_act[:, pl.ds(k * chans, chans)], 0.0)
    swap_v = swap(vx, vr, 9)

    sp_a, sp_b = spread_of(s0, s1, gain1)

    def body(j, _):
        at = rows_at(j, RC)
        normed = (xw[at, :].astype(F32) - mean1) * rstd1
        d = resid[at, :] + rstd1 * (tmp[at, :] * gain1 - mask2(j) * (sp_a + normed * sp_b))
        tmp[at, :] = d * own_f
        datt_s[at, :] = (d * own_f).astype(BF)
        return 0

    lax.fori_loop(0, px // RC, body, 0)
    swap_i = swap(datt_s.at[other_rows], ing_r, 10)
    step()

    swap_v.wait()
    vall[img] = vx[...] + vr[...]

    class Gather:
        def __init__(self):
            self.k = -1

        def advance(self):
            if self.k >= 0 and self.cp is not None:
                self.cp.wait()
                self.cp = None
            self.k += 1
            if self.k < nbits:
                bit = bits[self.k]
                at = vall.at[pl.ds((img // bit) * bit, bit)]
                base = used[0] + self.k
                self.cp = pltpu.make_async_remote_copy(
                    src_ref=at, dst_ref=at, send_sem=fs.at[base], recv_sem=fr.at[base],
                    device_id=(img + bit * (1 - 2 * ((img // bit) % 2)), c), device_id_type=MESH,
                )
                self.cp.start()
            else:
                self.cp = None

    running.append(Gather())

    swap_t.wait()
    res_out[...] = (tsum[my_rows, :] + trecv[...] + p_oo[...].reshape(1, -1)).astype(BF)
    step()
    swap_i.wait()
    tsum[pl.ds(0, half), :] = jnp.zeros((half, chans), F32)
    tsum[pl.ds(0, half), win] = tmp[my_rows, :]
    tsum[pl.ds(0, half), owin] += ing_r[...].astype(F32)
    ing_out[...] = tsum[pl.ds(0, half), :].astype(BF)

    for _ in range(2 * nbits + 2):
        step()
    for flow in running:
        if isinstance(flow, Flow):
            flow.wait_forward()
    outs = []
    for k, (src, dst) in enumerate(((out1, pk1_o), (out2, pk2_o), (outp, pp_o), (vall, vec_o))):
        cp = pltpu.make_async_copy(src, dst, lsem.at[k])
        cp.start()
        outs.append(cp)
    for cp in outs:
        cp.wait()


def finish_kernel(dims, pk1, pk2, pp, vec, *outs):
    chans, n_img, heads = dims
    (g1, s1, k1o, o1, ewo, eoo, g2, s2, k2o, o2, g3, s3, pio, oio, poo, ooo) = outs
    hc = chans // 2
    own = chans // 2

    for pay, out in ((pk1, k1o), (pk2, k2o)):

        def body(tap, _, pay=pay, out=out):
            at = pl.ds(pl.multiple_of(tap * chans, LANES), chans)
            out[at, pl.ds(0, LANES)] = pay[0, at, :].astype(F32)
            out[at, pl.ds(2 * LANES, LANES)] = pay[1, at, :].astype(F32)
            for s in range(2):
                src = pl.ds(pl.multiple_of(9 * chans + tap * hc, HEAD_DIM), hc)
                dst = pl.ds(pl.multiple_of(tap * chans + s * hc, HEAD_DIM), hc)
                out[dst, pl.ds(LANES, LANES)] = pay[s, src, :].astype(F32)
            return 0

        lax.fori_loop(0, 9, body, 0)

    width = 3 * heads * HEAD_DIM
    low = lax.broadcasted_iota(jnp.int32, (1, LANES), 1) < HEAD_DIM
    pairs = 3 * heads // 2
    for s in range(2):
        blocks = [pp[s, pl.ds(k * chans, chans), :].astype(F32) for k in range(pairs)]
        if (3 * heads) % 2:
            last = pp[s, pl.ds(pairs * chans, chans // 2), :].astype(F32)
            blocks.append(jnp.concatenate([last, pltpu.roll(last, HEAD_DIM, 1)], axis=0))
        if s == 0:
            first = blocks
        else:
            second = blocks
    cols = []
    if (3 * heads) % 2:
        cols = first[:-1]
        turned = [pltpu.roll(b, HEAD_DIM, 1) for b in second]
        cols.append(jnp.where(low, first[-1], turned[0]))
        for k in range(pairs):
            cols.append(jnp.where(low, turned[k], turned[k + 1]))
    else:
        cols = first + second
    for k, b in enumerate(cols):
        pio[:, pl.ds(k * LANES, LANES)] = b
    base = pairs * chans + ((3 * heads) % 2) * (chans // 2)
    for s in range(2):
        for b in range(chans // LANES):
            poo[pl.ds(s * own, own), pl.ds(b * LANES, LANES)] = pp[s, pl.ds(base + b * own, own), :].astype(F32)

    all_rows = vec[...]
    sums = jnp.sum(all_rows, axis=0)
    for out, k in ((g1, 0), (s1, 1), (o1, 2), (g2, 3), (s2, 4), (o2, 5), (g3, 6), (s3, 7), (ooo, 8)):
        out[...] = sums[k]
    for out, k in ((eoo, 9), (oio, 13)):
        out[pl.ds(0, chans)] = sums[k]
        out[pl.ds(chans, chans)] = sums[k + 1]
    for a in range(2):
        for b in range(2):
            ewo[pl.ds(a * chans, chans), pl.ds(b * chans, chans)] = lax.dot_general(
                vec[:, 11 + a, :], vec[:, 9 + b, :], (((0,), (0,)), ((), ())),
                preferred_element_type=F32, precision=lax.Precision.HIGHEST,
            )


def time_features(timesteps, width):
    half_width = width // 2
    frequency = jnp.exp(-math.log(10000.0) * jnp.arange(half_width, dtype=jnp.float32) / half_width)
    angles = timesteps.astype(jnp.float32)[:, None] * frequency[None, :]
    return jnp.concatenate([jnp.cos(angles), jnp.sin(angles)], axis=1)


def local(
    n_img,
    images_in, extents, timesteps, gain_first, shift_first, kernel_first, offset_first, embed_weight, embed_offset,
    gain_second, shift_second, kernel_second, offset_second, gain_attend, shift_attend, project_in, offset_in,
    project_out, offset_out, out_grad,
):
    _, stripe_rows, side, chans = images_in.shape
    px = side * side
    half = stripe_rows * side
    te = embed_weight.shape[0]
    own = chans // 2
    heads = own // HEAD_DIM
    taps = 9
    unit = 16 * n_img
    real_k = taps * chans + taps * (chans // 2)
    real_p = 3 * heads * HEAD_DIM * chans // LANES + own * (chans // LANES)
    rows_k = cdiv(real_k, unit) * unit
    rows_p = cdiv(real_p, unit) * unit
    bits = []
    while 2 ** len(bits) < n_img:
        bits.append(2 ** len(bits))
    nbits = len(bits)

    t_act = jax.nn.silu(time_features(timesteps, te))
    vm = pl.BlockSpec(memory_space=pltpu.VMEM)
    anym = pl.BlockSpec(memory_space=pl.ANY)
    smem = pl.BlockSpec(memory_space=pltpu.SMEM)
    sds = jax.ShapeDtypeStruct
    V = pltpu.VMEM
    padded = px + 2 * side
    wide = 3 * heads * LANES
    n_sem = 3 * 2 * (2 * nbits + 2) + nbits
    scratch = [
        V((taps * chans, chans), BF), V((taps * chans, chans), BF),
        V((chans + WIN - own, chans), BF), V((te, 2 * chans), BF), V((chans, wide), BF),
        V((px, WIN), BF), V((px, chans), BF), V((px, LANES), F32), V((1, 2 * chans), F32),
        V((2, padded, WIN), BF), V((2, padded, WIN), BF), V((2, px, WIN), BF), V((2, padded, WIN), BF), V((2, padded, WIN), BF),
        V((px, WIN), F32), V((px, WIN), F32), V((px, WIN), F32), V((px, WIN), F32),
        V((heads, px, LANES), BF), V((heads, px, LANES), BF), V((heads, px, LANES), BF),
        V((heads, LANES, px), BF), V((heads, LANES, px), BF), V((heads, LANES, px), BF), V((WIN, px), BF),
        V((heads, px, LANES), F32), V((heads, px, LANES), F32), V((heads, LANES, px), F32), V((px, wide), BF),
        V((px, chans), F32), V((half, chans), F32), V((px, WIN), BF), V((px, WIN), BF),
        V((3, padded, WIN), BF), V((chans, px), BF), V((half, WIN), BF),
        V((rows_k, LANES), BF), V((rows_k, LANES), BF), V((rows_p, LANES), BF),
        V((rows_k, LANES), BF), V((rows_k, LANES), BF), V((rows_p, LANES), BF),
        V((2, rows_k, LANES), BF), V((2, rows_k, LANES), BF), V((2, rows_p, LANES), BF),
        V((16, chans), F32), V((16, chans), F32), V((n_img, 16, chans), F32),
        pltpu.SemaphoreType.DMA((5,)), pltpu.SemaphoreType.DMA((11,)), pltpu.SemaphoreType.DMA((11,)),
        pltpu.SemaphoreType.DMA((n_sem,)), pltpu.SemaphoreType.DMA((n_sem,)),
    ]
    res, ing, pk1, pk2, pp, vec = pl.pallas_call(
        functools.partial(block_kernel, (side, chans, n_img, real_k, real_p, tuple(bits))),
        out_shape=(
            sds((half, chans), BF), sds((half, chans), BF), sds((2, rows_k, LANES), BF), sds((2, rows_k, LANES), BF),
            sds((2, rows_p, LANES), BF), sds((n_img, 16, chans), F32),
        ),
        in_specs=[vm, vm, smem] + [vm] * 12 + [anym, anym, anym, anym, anym],
        out_specs=(vm, vm, anym, anym, anym, anym),
        scratch_shapes=scratch,
        compiler_params=pltpu.CompilerParams(collective_id=0, has_side_effects=True, vmem_limit_bytes=60 * 2**20),
        cost_estimate=pl.CostEstimate(flops=2 * 10**10, bytes_accessed=2 * 10**7, transcendentals=4 * 10**6),
        name="block",
    )(
        images_in.reshape(half, chans), out_grad.reshape(half, chans), extents, gain_first, shift_first, offset_first,
        gain_second, shift_second, offset_second, gain_attend, shift_attend, offset_out, t_act, embed_offset, offset_in,
        kernel_first.reshape(taps * chans, chans), kernel_second.reshape(taps * chans, chans),
        project_in, project_out, embed_weight,
    )

    row = sds((chans,), F32)
    row2 = sds((2 * chans,), F32)
    kern = sds((taps * chans, chans), F32)
    outs = pl.pallas_call(
        functools.partial(finish_kernel, (chans, n_img, heads)),
        out_shape=(
            row, row, kern, row, sds((te, 2 * chans), F32), row2, row, row, kern, row, row, row,
            sds((chans, 3 * chans), F32), row2, sds((chans, chans), F32), row,
        ),
        in_specs=[vm] * 4,
        out_specs=(vm,) * 16,
        compiler_params=pltpu.CompilerParams(vmem_limit_bytes=60 * 2**20),
        name="finish",
    )(pk1, pk2, pp, vec)
    shapes = (
        gain_first, shift_first, kernel_first, offset_first, embed_weight, embed_offset, gain_second, shift_second,
        kernel_second, offset_second, gain_attend, shift_attend, project_in, offset_in, project_out, offset_out,
    )
    outs = [o.reshape(s.shape) for o, s in zip(outs, shapes)]
    return (res.reshape(images_in.shape), ing.reshape(images_in.shape), *outs)


def solution(mesh):
    n_img = mesh.shape["img"]
    stripe = P("img", "pix", None, None)
    in_specs = (stripe, P("img", None), P("img")) + (P(),) * 16 + (stripe,)
    out_specs = (stripe, stripe) + (P(),) * 16
    return jax.shard_map(
        functools.partial(local, n_img), mesh=mesh, in_specs=in_specs, out_specs=out_specs, check_vma=False
    )
```

time: 617 us -> 154 us (0.25); the launches traced: 605 us -> 153 us
  waiting for transfers between devices: 200 us -> 0 us
  Pallas kernels: 0 us -> 150 us
  local copies, waits for them, and re-layouts: 116 us -> 1.52 us
  matrix products: 84.3 us -> 0 us
  blocking collectives: 78.7 us -> 0 us
  other arithmetic: 71.2 us -> 0.65 us
  starting transfers between devices: 36.5 us -> 0 us
  between operations: 18 us -> 1.36 us
    psum x1 -> x0, waiting for transfers between devices: 200 us -> none  [local(): lax.psum((grad_gain_first, grad_shift_first, grad_kernel_first, grad_offs...]
    pallas_call x0 -> x2, Pallas kernels: none -> 150 us  [the longest x1 139 us: local(): pl.pallas_call(functools.partial(block_kernel, (side, chans, n_img, real_...]
    psum x7 -> x0, blocking collectives: 59.2 us -> none  [the longest x1 44.1 us: local(): lax.psum((grad_gain_first, grad_shift_first, grad_kernel_first, grad_offs...]
    dot_general x30 -> x0, matrix products: 58.5 us -> none  [the longest x18 24.5 us: kernel_grad(): lax.dot_general(window, flat_grad, (((0,), (0,)), ((), ())), preferred_el...]
    unnamed x176 -> x7, local copies, waits for them, and re-layouts: 48.5 us -> 1.51 us
    unnamed x4 -> x0, other arithmetic: 30.1 us -> none
    ppermute x12 -> x0, starting transfers between devices: 29.1 us -> none  [the longest x6 21.4 us: padded_2(): before = lax.ppermute(last, axis, up)]
    all_to_all x3 -> x0, blocking collectives: 19.5 us -> none  [the longest x1 6.88 us: local(): lax.all_to_all(qkv, 'pix', split_axis=2, concat_axis=1, tiled=True)]
  transfers between devices with their start and end apart: 15 -> 0, of which waited for: 1 -> 0; matrix products, arithmetic and copies ran while one was open for 9% -> 0% of each run, Pallas kernels for 0% -> 0%
where the time goes in v1:
time: 154 us; the launch traced here: 153 us
  Pallas kernels  150 us (97%)
    pallas_call x1, Pallas kernels, local(): pl.pallas_call(functools.partial(block_kernel, (side, chans, n_img, real_...  139 us
    pallas_call x1, Pallas kernels, local(): pl.pallas_call(functools.partial(finish_kernel, (chans, n_img, heads)), o...  11.3 us

profile of v1, /device:TPU:0, one launch (start us, length us, event | category | flops | bytes accessed | tf_op | source)
XLA Modules:
  0.0 153.3 jit_solution(10767315670565778258)
XLA Ops:
  1.4 0.6 divide_multiply_fusion.refs_12_
  2.0 138.5 %block.1 = (bf16[512,384]{1,0:T(8,128)(2,1)}, bf16[512,384]{1,0:T(8,128)(2,1)}, bf16[2,5376,128]{2,1,0:T(8,128)(2,1)}, bf16[2,5376,128]{2,1,0:T(8,128)(2,1)}, bf...) custom-call(bf16[512,384]{1,0:T(8,128)(2,1)} %bitcast.15, bf16[512,384]{1,0:T(8,128)(2,1)} %bitcast.16, ...), custom_call_target="tpu_custom_call" | custom-call | flops 20000000000 | bytes 20000000 | tf_op jit(solution)/shard_map/block/pallas_call | solution.py:864
  140.5 0.0 copy-start.1
  140.5 0.0 copy-start
  140.5 11.3 %finish.1 = (f32[384]{0:T(512)}, f32[384]{0:T(512)}, f32[3456,384]{1,0:T(8,128)}, f32[384]{0:T(512)}, f32[768,768]{1,0:T(8,128)}, /*index=5*/f32[768]{0:T(1024)}...) custom-call(bf16[2,5376,128]{2,1,0:T(8,128)(2,1)} %get-tuple-element, ...), custom_call_target="tpu_custom_call" | custom-call | tf_op jit(solution)/shard_map/finish/pallas_call | solution.py:886
  151.8 0.0 copy-done.1
  151.8 0.7 copy.42
  152.6 0.0 copy-done
  152.6 0.7 copy.43
  (3 shorter events, 0.1 us)
Async XLA Ops:
  140.5 11.3 %copy-start.1 = (bf16[512,384]{1,0:T(8,128)(2,1)S(1)}, bf16[512,384]{1,0:T(8,128)(2,1)}, u32[]{:S(2)}) copy-start(bf16[512,384]{1,0:T(8,128)(2,1)} %get-tuple-element.40) | copy-start | bytes 1179652
  140.5 12.1 %copy-start = (bf16[512,384]{1,0:T(8,128)(2,1)S(1)}, bf16[512,384]{1,0:T(8,128)(2,1)}, u32[]{:S(2)}) copy-start(bf16[512,384]{1,0:T(8,128)(2,1)} %get-tuple-element.41) | copy-start | bytes 1179652

commit v2 on v1

v2 whole, which is shorter than its diff:
```python
import functools
import math

import jax
import jax.numpy as jnp
from jax import lax
from jax.experimental import pallas as pl
from jax.experimental.pallas import tpu as pltpu
from jax.sharding import PartitionSpec as P

HEAD_DIM = 64
GROUPS = 32
EPSILON = 1e-05
MASKED = -1e30
BF = jnp.bfloat16
F32 = jnp.float32
MESH = pl.DeviceIdType.MESH
WIN = 256
LANES = 128
RC = 128
MC = 512
TC = 256
KERNEL_FLOWS = ((0, 4), (1, 4), (2, 3), (0, 4), (1, 3), (2, 3))
PROJECT_FLOWS = ((0, 3), (1, 3), (2, 3))
PLAN = (
    (0,),
    (2, 1),
    (3, 4, 5, 0),
    (2, 1),
    (4, 3, 5, 0),
    (13, 12),
    (2, 14, 1),
    (8, 6, 7, 4, 5, 3, 0, 12),
    (13, 2, 9, 10, 1, 14, 11, 8, 6, 7),
    (4, 5, 12),
    (3, 13, 0, 10, 9, 11, 14, 6, 2, 7, 8, 1),
    (4, 5, 10, 12, 11, 0, 2, 9, 1, 3, 4, 13, 5, 14, 6, 0, 7, 2, 8, 10, 1, 12, 3, 5, 11, 9, 4, 13, 14, 6, 0, 7, 8, 2, 13)
    + (10, 1, 11, 12, 3, 9, 7, 5, 10, 4, 14, 6, 8, 11, 13, 9, 12, 3, 7, 14, 6, 10, 8, 11, 13, 9, 12, 14, 8, 7, 6, 11, 10, 9),
)


def dot(a, b):
    return jnp.dot(a, b, preferred_element_type=F32)


def dot_nt(a, b):
    return lax.dot_general(a, b, (((1,), (1,)), ((), ())), preferred_element_type=F32)


def dot_hi(a, b):
    return jnp.dot(a, b, preferred_element_type=F32, precision=lax.Precision.HIGHEST)


def fold(v):
    return jnp.sum(v.reshape(v.shape[0] // 8, 8, v.shape[1]), axis=0)


def sigmoid(v):
    return 1.0 / (1.0 + jnp.exp(-v))


def cdiv(a, b):
    return -(-a // b)


def xor(img, bits, d):
    for pos, bit in enumerate(bits):
        if (d >> pos) & 1:
            img = img + bit * (1 - 2 * ((img // bit) % 2))
    return img


def index_in(img, bits, d=0):
    v = 0
    for pos, bit in enumerate(bits):
        mine = (img // bit) % 2
        v = v + ((1 - mine) if (d >> pos) & 1 else mine) * (1 << pos)
    return v


def shares(total, flows):
    weight = sum(w for _, w in flows)
    ends = [0]
    for k in range(len(flows)):
        ends.append(-(-total * sum(w for _, w in flows[: k + 1]) // weight))
    return [b - a for a, b in zip(ends, ends[1:])]


class Flow:
    def __init__(self, pay, rbuf, out, base, rows, stages, sems, core, img):
        self.pay, self.rbuf, self.out, self.lo, self.size = pay, rbuf, out, base, rows
        self.base, self.rows = base, rows
        self.rbase, self.stages, self.sems, self.core, self.img = base, stages, sems, core, img
        self.k = -1
        self.used = 0
        self.copies = []
        self.forwards = []

    def send(self, src, dst, device):
        send, recv, first = self.sems
        cp = pltpu.make_async_remote_copy(
            src_ref=src, dst_ref=dst, send_sem=send.at[first + self.used], recv_sem=recv.at[first + self.used],
            device_id=device, device_id_type=MESH,
        )
        self.used += 1
        cp.start()
        return cp

    def forward(self, lo, size):
        ref = self.out.at[self.core, pl.ds(pl.multiple_of(lo, 16), size)]
        self.forwards.append(self.send(ref, ref, (self.img, 1 - self.core)))

    def start(self):
        n = len(self.stages)
        self.copies = []
        if self.k < n:
            bits = self.stages[self.k]
            part = self.size >> len(bits)
            for d in range(1, 1 << len(bits)):
                lo = pl.multiple_of(self.lo + index_in(self.img, bits, d) * part, 16)
                src = self.pay.at[pl.ds(lo, part)]
                dst = self.rbuf.at[pl.ds(self.rbase + (d - 1) * part, part)]
                self.copies.append(self.send(src, dst, (xor(self.img, bits, d), self.core)))
        else:
            bits = self.stages[2 * n - 1 - self.k]
            ref = self.out.at[self.core, pl.ds(self.lo, self.size)]
            for d in range(1, 1 << len(bits)):
                self.copies.append(self.send(ref, ref, (xor(self.img, bits, d), self.core)))
            if self.k == 2 * n - 1:
                self.forward(self.lo, self.size)

    def finish(self):
        n = len(self.stages)
        for cp in self.copies:
            cp.wait()
        if self.k < n:
            bits = self.stages[self.k]
            more = (1 << len(bits)) - 1
            part = self.size >> len(bits)
            keep = pl.multiple_of(self.lo + index_in(self.img, bits) * part, 16)
            rbase = self.rbase
            step = 16
            for cand in (512, 448, 256, 128, 112, 64, 48, 32):
                if part % cand == 0:
                    step = cand
                    break

            def add(j, _):
                at = pl.ds(pl.multiple_of(keep + j * step, 16), step)
                v = self.pay[at, :].astype(F32)
                for d in range(more):
                    v = v + self.rbuf[pl.ds(pl.multiple_of(rbase + d * part + j * step, 16), step), :].astype(F32)
                if self.k == n - 1:
                    self.out[self.core, at, :] = v.astype(BF)
                else:
                    self.pay[at, :] = v.astype(BF)
                return 0

            lax.fori_loop(0, part // step, add, 0)
            self.lo, self.size = keep, part
            self.rbase += more * part
        else:
            bits = self.stages[2 * n - 1 - self.k]
            mine = index_in(self.img, bits)
            whole = pl.multiple_of(self.lo - mine * self.size, 16)
            if self.k == 2 * n - 1:
                for d in range(1, 1 << len(bits)):
                    self.forward(whole + index_in(self.img, bits, d) * self.size, self.size)
            self.lo = whole
            self.size <<= len(bits)

    def ended(self):
        return self.k >= 2 * len(self.stages)

    def advance(self):
        last = 2 * len(self.stages)
        if self.ended():
            return
        if self.k >= 0:
            self.finish()
        self.k += 1
        if self.k < last:
            self.start()


def block_kernel(dims, *refs):
    side, chans, n_img, real_k, real_p, bits, flow_sems = dims
    (
        x_in, g_in, ext, p_g1, p_s1, p_o1, p_g2, p_s2, p_o2, p_g3, p_s3, p_oo, t_act, e_off, off_in, k1_h, k2_h, wi_h, wo_h, ew_h,
        res_out, ing_out, pk1_o, pk2_o, pp_o, vec_o,
        k1, k2, wo, ew, wq, xw, gf, mask, film, act1, act2, act3, dd2, dd1,
        cv, hid, tmp, resid, qa, ka, va, kat, vat, dot_t, att_t, dqkv,
        tsum, trecv, datt_s, datt_r, dm, act_t1, act_t2, act_t3, ing_r, tsum_i,
        pay1, pay2, payp, rb1, rb2, rbp, out1, out2, outp, vx, vr, vall,
        lsem, os, xs, xr, fs, fr,
    ) = refs
    img = lax.axis_index("img")
    c = lax.axis_index("pix")
    oc = 1 - c
    px = side * side
    half = px // 2
    own_chans = chans // 2
    heads = own_chans // HEAD_DIM
    first = c == 0
    nbits = len(bits)

    def aligned(v, m):
        return pl.multiple_of(v, m)

    def rows_at(j, size):
        return pl.ds(aligned(j * size, size), size)

    def pad_at(j, size, shift=side):
        return pl.ds(aligned(j * size + shift, 32), size)

    win = pl.ds(aligned(LANES * c, LANES), WIN)
    owin = pl.ds(aligned(LANES * oc, LANES), WIN)

    barrier = pltpu.get_barrier_semaphore()
    peers = [(img, oc)]
    turns = []
    for r in range(3):
        near = list(bits[:3])[r:] + list(bits[:3])[:r]
        turns.append([[bit] for bit in near + list(bits[3:])])
    for bit in bits:
        peers.append((xor(img, [bit], 1), c))
    for peer in peers:
        pl.semaphore_signal(barrier, inc=1, device_id=peer, device_id_type=MESH)

    loads = []
    my_rows = pl.ds(aligned(half * c, half), half)
    other_rows = pl.ds(aligned(half * oc, half), half)
    copies = (
        (x_in.at[:, win], xw.at[my_rows]),
        (k1_h, k1),
        (g_in, gf.at[my_rows]),
        (ew_h, ew),
        (wi_h, dqkv.at[pl.ds(0, chans)]),
        (wo_h, wo.at[pl.ds(0, chans)]),
        (k2_h, k2),
    )
    for k, (src, dst) in enumerate(copies):
        cp = pltpu.make_async_copy(src, dst, lsem.at[k])
        cp.start()
        loads.append(cp)
    load_x, load_k1, load_g, load_ew, load_wi, load_wo, load_k2 = loads
    pl.semaphore_wait(barrier, len(peers))

    def swap(src, dst, k):
        cp = pltpu.make_async_remote_copy(
            src_ref=src, dst_ref=dst, send_sem=xs.at[k], recv_sem=xr.at[k], device_id=(img, oc), device_id_type=MESH
        )
        cp.start()
        return cp

    swap_x = swap(x_in.at[:, owin], xw.at[my_rows], 0)
    swap_g = swap(g_in, gf.at[my_rows], 1)

    lane = lax.broadcasted_iota(jnp.int32, (1, WIN), 1)
    own_f = (jnp.where(first, lane, WIN - 1 - lane) < own_chans).astype(F32)
    rows_e = ext[0, 0]
    cols_e = ext[0, 1]
    per = chans // GROUPS
    inv_entries = 1.0 / jnp.full((1, WIN), rows_e * cols_e * per, jnp.int32).astype(F32)
    gi = lax.broadcasted_iota(jnp.int32, (WIN, WIN), 0) + LANES * c
    gj = lax.broadcasted_iota(jnp.int32, (WIN, WIN), 1) + LANES * c
    same = (gi // per == gj // per).astype(F32)

    def pvec(ref):
        return ref[win].reshape(1, WIN)

    gain1, shift1, offset1 = pvec(p_g1), pvec(p_s1), pvec(p_o1)
    gain2, shift2, offset2 = pvec(p_g2), pvec(p_s2), pvec(p_o2)
    gain3, shift3 = pvec(p_g3), pvec(p_s3)

    def group_totals(a, b):
        both = dot_hi(jnp.concatenate([a, b], axis=0), same)
        return jnp.sum(both[:8], axis=0, keepdims=True), jnp.sum(both[8:], axis=0, keepdims=True)

    def total(a):
        return jnp.sum(a, axis=0, keepdims=True)

    zero8 = jnp.zeros((8, WIN), F32)

    def fill_mask(j, _):
        p = lax.broadcasted_iota(jnp.int32, (RC, LANES), 0) + j * RC
        ok = (p // side < rows_e) & (p % side < cols_e)
        mask[rows_at(j, RC), :] = ok.astype(F32)
        return 0

    lax.fori_loop(0, px // RC, fill_mask, 0)

    def mask2(j, size=RC):
        m = mask[rows_at(j, size), :]
        return jnp.concatenate([m, m], axis=1)

    edge = jnp.zeros((side, WIN), BF)
    for buf in (act1, act2, dd2, dd1):
        for s in range(2):
            buf[s, pl.ds(0, side), :] = edge
            buf[s, pl.ds(side + px, side), :] = edge
    for b in range(3):
        dm[b, pl.ds(0, side), :] = edge
        dm[b, pl.ds(side + px, side), :] = edge
    for pay, real in ((pay1, real_k), (pay2, real_k), (payp, real_p)):
        rest = pay.shape[0] - real
        if rest:
            pay[pl.ds(real, rest), :] = jnp.zeros((rest, LANES), BF)
    wo[pl.ds(chans, WIN - own_chans), :] = jnp.zeros((WIN - own_chans, chans), BF)
    for h in range(heads):
        dot_t[h, pl.ds(HEAD_DIM, HEAD_DIM), :] = jnp.zeros((HEAD_DIM, px), BF)
    att_t[pl.ds(own_chans, WIN - own_chans), :] = jnp.zeros((WIN - own_chans, px), BF)
    vx[...] = jnp.zeros(vx.shape, F32)

    def stats_step(v, m, carry):
        vm = v * m
        return carry[0] + fold(vm), carry[1] + fold(vm * v)

    def moments(carry):
        s, q = group_totals(*carry)
        mean = s * inv_entries
        return mean, lax.rsqrt(q * inv_entries - mean * mean + EPSILON)

    def body(j, carry, at=0):
        j = j + at
        return stats_step(xw[rows_at(j, RC), :].astype(F32), mask2(j), carry)

    steps = half // RC
    load_x.wait()
    carry = lax.fori_loop(0, steps, functools.partial(body, at=steps * c), (zero8, zero8))
    swap_x.wait()
    mean1, rstd1 = moments(lax.fori_loop(0, steps, functools.partial(body, at=steps * oc), carry))
    mul1 = rstd1 * gain1
    add1 = shift1 - mean1 * mul1

    def body(j, _):
        pre = xw[rows_at(j, RC), :].astype(F32) * mul1 + add1
        act1[c, pad_at(j, RC), :] = (pre * sigmoid(pre) * own_f).astype(BF)
        return 0

    lax.fori_loop(0, px // RC, body, 0)
    inner = pl.ds(side, px)
    swap_a1 = swap(act1.at[c, inner], act1.at[c, inner], 2)

    col = lax.broadcasted_iota(jnp.int32, (MC, WIN), 0) % side
    not_first = (col != 0).astype(F32)
    not_last = (col != side - 1).astype(F32)

    def conv(acts, s, kern, back, j):
        accs = []
        for b in range(3):
            acc = None
            for a in range(3):
                lhs = acts[s, pl.ds(aligned(j * MC + side * a, 32), MC), :]
                if back:
                    tap = (2 - a) * 3 + 2 - b
                    rhs = kern[pl.ds(aligned(tap * chans + LANES * c, LANES), WIN), pl.ds(aligned(LANES * s, LANES), WIN)]
                    o = dot_nt(lhs, rhs)
                else:
                    tap = a * 3 + b
                    rhs = kern[pl.ds(aligned(tap * chans + LANES * s, LANES), WIN), win]
                    o = dot(lhs, rhs)
                acc = o if acc is None else acc + o
            accs.append(acc)
        return accs[1] + pltpu.roll(accs[0], 1, 0) * not_first + pltpu.roll(accs[2], MC - 1, 0) * not_last

    def turn(acts, shift, dst):
        def body(j, _):
            a0 = acts[0, pad_at(j, TC, shift), :].astype(F32)
            a1 = acts[1, pad_at(j, TC, shift), :].astype(F32)
            at = rows_at(j, TC)
            dst[pl.ds(0, LANES), at] = a0[:, :LANES].T.astype(BF)
            dst[pl.ds(LANES, LANES), at] = (a0[:, LANES:] + a1[:, :LANES]).T.astype(BF)
            dst[pl.ds(2 * LANES, LANES), at] = a1[:, LANES:].T.astype(BF)
            return 0

        lax.fori_loop(0, px // TC, body, 0)

    load_k1.wait()

    def body(j, _):
        cv[rows_at(j, MC), :] = conv(act1, c, k1, False, j)
        return 0

    lax.fori_loop(0, px // MC, body, 0)
    lane1 = lax.broadcasted_iota(jnp.int32, (1, LANES), 1)
    low1 = lane1 < HEAD_DIM
    load_wi.wait()
    for k in range(3 * heads):
        place = 3 * heads * c + k
        blk = dqkv[pl.ds(0, chans), pl.ds(aligned((place // 2) * LANES, LANES), LANES)].astype(F32)
        blk = jnp.where(place % 2 == 0, blk, pltpu.roll(blk, HEAD_DIM, 1))
        wq[:, pl.ds(k * LANES, LANES)] = jnp.where(low1, blk, 0.0).astype(BF)

    load_ew.wait()
    t = t_act[...]
    t_a = t.astype(BF).astype(F32)
    t_b = (t - t_a).astype(BF).astype(F32)
    row16 = lax.broadcasted_iota(jnp.int32, (16, t.shape[1]), 0)
    t_rows = jnp.where(row16 == 0, t_a, jnp.where(row16 == 1, t_b, jnp.where(row16 == 2, t - t_a - t_b, 0.0)))
    film[...] = total(dot(t_rows.astype(BF), ew[...])) + e_off[...].reshape(1, -1)
    scale2 = 1.0 + film[:, win]
    move2 = film[:, pl.ds(aligned(chans + LANES * c, LANES), WIN)]

    swap_a1.wait()

    def body(j, carry):
        v = cv[rows_at(j, MC), :] + conv(act1, oc, k1, False, j) + offset1
        cv[rows_at(j, MC), :] = v
        return stats_step(v, mask2(j, MC), carry)

    mean2, rstd2 = moments(lax.fori_loop(0, px // MC, body, (zero8, zero8)))
    mul2 = rstd2 * gain2 * scale2
    add2 = (shift2 - mean2 * rstd2 * gain2) * scale2 + move2

    def body(j, _):
        pre = cv[rows_at(j, RC), :] * mul2 + add2
        act2[c, pad_at(j, RC), :] = (pre * sigmoid(pre) * own_f).astype(BF)
        return 0

    lax.fori_loop(0, px // RC, body, 0)
    swap_a2 = swap(act2.at[c, inner], act2.at[c, inner], 3)

    load_k2.wait()

    def body(j, _):
        at = rows_at(j, MC)
        hid[at, :] = conv(act2, c, k2, False, j) + offset2 + xw[at, :].astype(F32)
        return 0

    lax.fori_loop(0, px // MC, body, 0)
    swap_a2.wait()

    def body(j, carry):
        v = hid[rows_at(j, MC), :] + conv(act2, oc, k2, False, j)
        hid[rows_at(j, MC), :] = v
        return stats_step(v, mask2(j, MC), carry)

    mean3, rstd3 = moments(lax.fori_loop(0, px // MC, body, (zero8, zero8)))
    mul3 = rstd3 * gain3
    add3 = shift3 - mean3 * mul3

    def body(j, _):
        act3[c, rows_at(j, RC), :] = ((hid[rows_at(j, RC), :] * mul3 + add3) * own_f).astype(BF)
        return 0

    lax.fori_loop(0, px // RC, body, 0)
    swap_a3 = swap(act3.at[c], act3.at[c], 4)

    biases = []
    for h in range(heads):
        blk = off_in[pl.ds(aligned(LANES * (heads * c + h), LANES), LANES)].reshape(1, LANES)
        turned = pltpu.roll(jnp.broadcast_to(blk, (8, LANES)), HEAD_DIM, 1)[:1]
        bias_q = jnp.where(low1, blk, jnp.where(lane1 == HEAD_DIM, 8.0, 0.0))
        bias_v = jnp.where(low1, turned, jnp.where(lane1 < HEAD_DIM + 2, 1.0, 0.0))
        biases.append((bias_q, bias_v))
    load_wo.wait()
    load_g.wait()
    swap_g.wait()
    wo_rows = pl.ds(aligned(own_chans * c, HEAD_DIM), own_chans)

    def body(j, _):
        o = dot_nt(wo[wo_rows, :], gf[rows_at(j, MC), :])
        for h in range(heads):
            dot_t[h, pl.ds(0, HEAD_DIM), rows_at(j, MC)] = o[HEAD_DIM * h : HEAD_DIM * (h + 1)].astype(BF)
        return 0

    lax.fori_loop(0, px // MC, body, 0)

    turn(act1, side, act_t1)
    turn(act2, side, act_t2)
    swap_a3.wait()

    def body(j, _):
        at = rows_at(j, MC)
        a0 = act3[0, at, :]
        a1 = act3[1, at, :]
        hidden_key = (mask[at, :] == 0.0) & (lane1 == HEAD_DIM)
        for h in range(heads):
            cols = pl.ds(3 * LANES * h, 3 * LANES)
            o = dot(a0, wq[pl.ds(0, WIN), cols]) + dot(a1, wq[pl.ds(LANES, WIN), cols])
            q = (o[:, :LANES] + biases[h][0]).astype(BF).astype(F32) * 0.125
            k = jnp.where(hidden_key, MASKED, o[:, LANES : 2 * LANES])
            v = o[:, 2 * LANES :] + biases[h][1]
            qa[h, at, :] = q.astype(BF)
            ka[h, at, :] = k.astype(BF)
            va[h, at, :] = v.astype(BF)
            kat[h, :, at] = k.T.astype(BF)
            vat[h, :, at] = v.T.astype(BF)
        return 0

    lax.fori_loop(0, px // MC, body, 0)

    row128 = lax.broadcasted_iota(jnp.int32, (LANES, px), 0)

    def body(h, _):
        qc = qa[h]
        scores = dot_nt(ka[h], qc)
        top = jnp.max(scores, axis=0, keepdims=True)
        e = jnp.exp(scores - top).astype(BF)
        o = dot(vat[h], e)
        inv = 1.0 / o[HEAD_DIM : HEAD_DIM + 1, :]
        o = o * inv
        att_t[pl.ds(aligned(HEAD_DIM * h, HEAD_DIM), HEAD_DIM), :] = o[:HEAD_DIM].astype(BF)
        g = dot_t[h].astype(F32)
        less = -inv * jnp.sum(g * o, axis=0, keepdims=True)
        high = less.astype(BF).astype(F32)
        g = jnp.where(row128 == HEAD_DIM, high, jnp.where(row128 == HEAD_DIM + 1, less - high, g * inv)).astype(BF)
        ds = (e.astype(F32) * dot(va[h], g)).astype(BF)
        grads = (dot(kat[h], ds).T * 0.125, dot(ds, qc), dot_nt(e, g))
        for k, d in enumerate(grads):
            dqkv[:, pl.ds(aligned((3 * h + k) * LANES, LANES), LANES)] = jnp.where(low1, d, 0.0).astype(BF)
        return 0

    lax.fori_loop(0, heads, body, 0)

    def body(j, _):
        at = rows_at(j, MC)
        datt_s[at, :] = dot_nt(dqkv[at, :], wq[owin, :]).astype(BF)
        return 0

    lax.fori_loop(0, px // MC, body, 0)
    swap_da = swap(datt_s, datt_r, 5)

    def body(j, _):
        at = rows_at(j, MC)
        tmp[at, :] = dot_nt(dqkv[at, :], wq[win, :])
        return 0

    lax.fori_loop(0, px // MC, body, 0)
    turn(act3, 0, act_t3)

    used = [0]
    flows = {}

    def flow_of(key, pay, rbuf, gathered, dst, k, base, size):
        if size:
            flow = Flow(pay, rbuf, gathered, base, size, turns[k], (fs, fr, used[0]), c, img)
            flow.dst = dst
            used[0] += flow_sems
            flows[key] = flow
            flow.advance()

    def advance(point):
        for key in PLAN[point]:
            if key in flows:
                flows[key].advance()

    stores = []

    def store(src, dst):
        cp = pltpu.make_async_copy(src, dst, os.at[len(stores)])
        cp.start()
        stores.append(cp)

    def hand_out(key):
        flow = flows.pop(key)
        for cp in flow.forwards:
            cp.wait()
        at = pl.ds(flow.base, flow.rows)
        store(flow.out.at[:, at], flow.dst.at[:, at])

    swap_da.wait()

    def back_sums(carry, u, normed):
        return carry[0] + fold(u), carry[1] + fold(u * normed)

    def body(j, carry):
        at = rows_at(j, RC)
        u = tmp[at, :] + datt_r[at, :].astype(F32)
        tmp[at, :] = u
        return back_sums(carry, u, (hid[at, :] - mean3) * rstd3)

    s0, s1 = lax.fori_loop(0, px // RC, body, (zero8, zero8))
    vx[pl.ds(6, 1), win] = total(s1) * own_f
    vx[pl.ds(7, 1), win] = total(s0) * own_f

    def spread_of(s0, s1, gain):
        a, b = group_totals(s0 * gain, s1 * gain)
        return a * inv_entries, b * inv_entries

    sp_a, sp_b = spread_of(s0, s1, gain3)

    def body(j, carry):
        at = rows_at(j, RC)
        normed = (hid[at, :] - mean3) * rstd3
        d = gf[at, win].astype(F32) + rstd3 * (tmp[at, :] * gain3 - mask2(j) * (sp_a + normed * sp_b))
        resid[at, :] = d
        low = (d * own_f).astype(BF)
        dd2[c, pad_at(j, RC), :] = low
        return carry + fold(low.astype(F32))

    vx[pl.ds(5, 1), win] = total(lax.fori_loop(0, px // RC, body, zero8))
    swap_d2 = swap(dd2.at[c, inner], dd2.at[c, inner], 7)

    def body(j, _):
        tmp[rows_at(j, MC), :] = conv(dd2, c, k2, True, j)
        return 0

    lax.fori_loop(0, px // MC, body, 0)
    swap_d2.wait()

    def shifted(dd):
        def body(j, _):
            d = dd[c, pad_at(j, TC), :].astype(F32)
            mid = dd[oc, pad_at(j, TC), pl.ds(aligned(LANES * c, LANES), LANES)].astype(F32)
            none = jnp.zeros((TC, LANES), F32)
            d = d + jnp.where(first, jnp.concatenate([none, mid], axis=1), jnp.concatenate([mid, none], axis=1))
            at = pad_at(j, TC)
            dm[0, at, :] = (pltpu.roll(d, TC - 1, 0) * not_last[:TC]).astype(BF)
            dm[1, at, :] = d.astype(BF)
            dm[2, at, :] = (pltpu.roll(d, 1, 0) * not_first[:TC]).astype(BF)
            return 0

        lax.fori_loop(0, px // TC, body, 0)

    def kernel_grad(act_t, key, pay, rbuf, gathered, dst, points):
        hc = chans // 2
        unit = 16 * n_img

        def body(tap, _):
            a = tap // 3
            b = tap % 3
            o = dot(act_t[...], dm[b, pl.ds(aligned(side * (2 - a), 32), px), :])
            lo, hi = o[:, :LANES], o[:, LANES:]
            main = jnp.where(first, lo, hi)
            mid = jnp.where(first, hi[:hc], lo[hc:])
            at = tap * (chans + hc)
            pay[pl.ds(aligned(at, HEAD_DIM), chans), :] = main.astype(BF)
            pay[pl.ds(aligned(at + chans, HEAD_DIM), hc), :] = mid.astype(BF)
            return 0

        done = 0
        base = 0
        for k, units in enumerate(shares(pay.shape[0] // unit, KERNEL_FLOWS)):
            need = min(9, cdiv(base + units * unit, chans + hc))
            if need > done:
                lax.fori_loop(done, need, body, 0)
                done = need
            flow_of(key + k, pay, rbuf, gathered, dst, KERNEL_FLOWS[k][0], base, units * unit)
            base += units * unit
            if k in points:
                advance(points[k])

    shifted(dd2)
    kernel_grad(act_t2, 0, pay2, rb2, out2, pk2_o, {})

    def body(j, carry):
        at = rows_at(j, MC)
        pre = cv[at, :] * mul2 + add2
        sg = sigmoid(pre)
        u = (tmp[at, :] + conv(dd2, oc, k2, True, j)) * (sg * (1.0 + pre * (1.0 - sg)))
        tmp[at, :] = u
        return back_sums(carry, u, (cv[at, :] - mean2) * rstd2)

    s0, s1 = lax.fori_loop(0, px // MC, body, (zero8, zero8))
    advance(0)
    t0, t1 = total(s0), total(s1)
    vx[pl.ds(9, 1), win] = (gain2 * t1 + shift2 * t0) * own_f
    vx[pl.ds(10, 1), win] = t0 * own_f
    vx[pl.ds(3, 1), win] = scale2 * t1 * own_f
    vx[pl.ds(4, 1), win] = scale2 * t0 * own_f
    gain2s = gain2 * scale2
    sp_a, sp_b = spread_of(s0, s1, gain2s)

    def body(j, carry):
        at = rows_at(j, RC)
        normed = (cv[at, :] - mean2) * rstd2
        d = rstd2 * (tmp[at, :] * gain2s - mask2(j) * (sp_a + normed * sp_b))
        low = (d * own_f).astype(BF)
        dd1[c, pad_at(j, RC), :] = low
        return carry + fold(low.astype(F32))

    vx[pl.ds(2, 1), win] = total(lax.fori_loop(0, px // RC, body, zero8))
    swap_d1 = swap(dd1.at[c, inner], dd1.at[c, inner], 8)

    advance(1)

    for k in range(3 * heads // 2):
        o = dot(act_t3[...], dqkv[:, pl.ds(2 * LANES * k, 2 * LANES)])
        pair = o[:, :LANES] + pltpu.roll(o[:, LANES:], HEAD_DIM, 1)
        payp[pl.ds(k * chans, chans), :] = pair.astype(BF)
    base = (3 * heads // 2) * chans
    if (3 * heads) % 2:
        o = dot(act_t3[...], dqkv[:, pl.ds((3 * heads - 1) * LANES, LANES)])
        pair = o[: chans // 2] + pltpu.roll(o[chans // 2 :], HEAD_DIM, 1)
        payp[pl.ds(base, chans // 2), :] = pair.astype(BF)
        base += chans // 2
    o = dot(att_t[pl.ds(0, own_chans), :], gf[...])
    for b in range(chans // LANES):
        payp[pl.ds(base + b * own_chans, own_chans), :] = o[:, b * LANES : (b + 1) * LANES].astype(BF)

    for h in range(heads):
        z = jnp.zeros((8, LANES), F32)

        def body(j, carry, h=h):
            at = rows_at(j, TC)
            q = dqkv[at, pl.ds(3 * h * LANES, LANES)].astype(F32)
            v = dqkv[at, pl.ds((3 * h + 2) * LANES, LANES)].astype(F32)
            return carry[0] + fold(q), carry[1] + fold(v)

        sum_q, sum_v = lax.fori_loop(0, px // TC, body, (z, z))
        sums = total(sum_q + pltpu.roll(sum_v, HEAD_DIM, 1))
        vx[pl.ds(13, 1), pl.ds(LANES * h, LANES)] = jnp.where(first, sums, 0.0)
        vx[pl.ds(14, 1), pl.ds(LANES * h, LANES)] = jnp.where(first, 0.0, sums)

    advance(2)
    at = 0
    for k, units in enumerate(shares(payp.shape[0] // (16 * n_img), PROJECT_FLOWS)):
        flow_of(12 + k, payp, rbp, outp, pp_o, PROJECT_FLOWS[k][0], at, units * 16 * n_img)
        at += units * 16 * n_img

    swap_d1.wait()
    shifted(dd1)
    advance(3)
    kernel_grad(act_t1, 6, pay1, rb1, out1, pk1_o, {2: 4, 3: 5, 4: 6})

    def body(j, _):
        tmp[rows_at(j, MC), :] = conv(dd1, c, k1, True, j)
        return 0

    lax.fori_loop(0, px // MC, body, 0)
    advance(7)

    def body(j, carry):
        at = rows_at(j, MC)
        x = xw[at, :].astype(F32)
        pre = x * mul1 + add1
        sg = sigmoid(pre)
        u = (tmp[at, :] + conv(dd1, oc, k1, True, j)) * (sg * (1.0 + pre * (1.0 - sg)))
        tmp[at, :] = u
        return back_sums(carry, u, (x - mean1) * rstd1)

    s0, s1 = lax.fori_loop(0, px // MC, body, (zero8, zero8))
    advance(8)
    vx[pl.ds(0, 1), win] = total(s1) * own_f
    vx[pl.ds(1, 1), win] = total(s0) * own_f

    g_sum = jnp.zeros((8, chans), F32)

    def body(j, carry):
        return carry + fold(gf[rows_at(j, RC), :].astype(F32))

    g_sum = total(lax.fori_loop(0, px // RC, body, g_sum))
    vx[pl.ds(8, 1), :] = jnp.where(first, g_sum, 0.0)
    for k in range(2):
        vx[pl.ds(11 + k, 1), :] = jnp.where(first, t_act[:, pl.ds(k * chans, chans)], 0.0)
    swap_v = swap(vx, vr, 9)

    sp_a, sp_b = spread_of(s0, s1, gain1)

    def body(j, _):
        at = rows_at(j, RC)
        normed = (xw[at, :].astype(F32) - mean1) * rstd1
        d = resid[at, :] + rstd1 * (tmp[at, :] * gain1 - mask2(j) * (sp_a + normed * sp_b))
        tmp[at, :] = d * own_f
        datt_s[at, :] = (d * own_f).astype(BF)
        return 0

    lax.fori_loop(0, px // RC, body, 0)
    swap_i = swap(datt_s.at[other_rows], ing_r, 10)

    swap_v.wait()
    vall[img] = vx[...] + vr[...]

    class Gather:
        def __init__(self):
            self.k = -1
            self.copies = []

        def advance(self):
            for cp in self.copies:
                cp.wait()
            self.copies = []
            self.k += 1
            if self.k < nbits:
                bit = bits[self.k]
                at = vall.at[pl.ds((img // bit) * bit, bit)]
                k = used[0]
                used[0] += 1
                cp = pltpu.make_async_remote_copy(
                    src_ref=at, dst_ref=at, send_sem=fs.at[k], recv_sem=fr.at[k],
                    device_id=(xor(img, [bit], 1), c), device_id_type=MESH,
                )
                cp.start()
                self.copies.append(cp)

    vectors = Gather()
    vectors.advance()
    advance(9)

    def body(j, _):
        at = rows_at(j, TC)
        tsum[at, :] = dot(att_t[:, at].astype(F32).T.astype(BF), wo[pl.ds(aligned(own_chans * c, HEAD_DIM), WIN), :])
        tsum[at, win] += hid[at, :] * own_f
        return 0

    lax.fori_loop(0, px // TC, body, 0)
    swap_t = swap(tsum.at[other_rows], trecv, 6)

    advance(10)
    vectors.advance()

    swap_i.wait()
    tsum_i[...] = jnp.zeros((half, chans), F32)
    tsum_i[:, win] = tmp[my_rows, :]
    tsum_i[:, owin] += ing_r[...].astype(F32)
    ing_out[...] = tsum_i[...].astype(BF)
    swap_t.wait()
    res_out[...] = (tsum[my_rows, :] + trecv[...] + p_oo[...].reshape(1, -1)).astype(BF)
    ended = {}
    for n, key in enumerate(PLAN[11]):
        if key in flows:
            flows[key].advance()
            if flows[key].ended():
                ended.setdefault(key, n)
        if n % 8 == 7:
            vectors.advance()
        for key in [k for k in ended if ended[k] + 6 == n]:
            hand_out(key)
    while any(not flow.ended() for flow in flows.values()):
        for flow in flows.values():
            flow.advance()
        vectors.advance()
    while vectors.copies:
        vectors.advance()
    store(vall, vec_o)
    for key in sorted(flows, key=lambda k: ended.get(k, 0)):
        hand_out(key)
    for cp in stores:
        cp.wait()


def finish_kernel(dims, pk1, pk2, pp, vec, res, ing, *refs):
    chans, heads = dims
    (res_o, ing_o, g1, s1, k1o, o1, ewo, eoo, g2, s2, k2o, o2, g3, s3, pio, oio, poo, ooo) = refs[:18]
    (b1, b2, bp, bv, br, f1, f2, fe, fi, fo, isem, osem) = refs[18:]
    hc = chans // 2
    own = chans // 2
    te = fe.shape[0]

    def move(src, dst, sem):
        cp = pltpu.make_async_copy(src, dst, sem)
        cp.start()
        return cp

    each = 3 * (chans + hc)
    get_2 = [move(pk2.at[:, pl.ds(a * each, each)], b2.at[:, pl.ds(a * each, each)], isem.at[a]) for a in range(3)]
    get_v = move(vec, bv, isem.at[3])
    get_1 = [move(pk1.at[:, pl.ds(a * each, each)], b1.at[:, pl.ds(a * each, each)], isem.at[4 + a]) for a in range(3)]
    get_p = move(pp, bp, isem.at[7])
    get_r = [move(src, br.at[k], isem.at[8 + k]) for k, src in enumerate((res, ing))]
    out = []

    def kernel(n, pay, get, full, dst):
        for a in range(3):
            get[a].wait()

            def body(b, _, a=a):
                tap = 3 * a + b
                src = tap * (chans + hc)
                at = pl.ds(pl.multiple_of(tap * chans, LANES), chans)
                main = pl.ds(pl.multiple_of(src, HEAD_DIM), chans)
                full[at, pl.ds(0, LANES)] = pay[0, main, :].astype(F32)
                full[at, pl.ds(2 * LANES, LANES)] = pay[1, main, :].astype(F32)
                mid = pl.ds(pl.multiple_of(src + chans, HEAD_DIM), hc)
                for s in range(2):
                    to = pl.ds(pl.multiple_of(tap * chans + s * hc, HEAD_DIM), hc)
                    full[to, pl.ds(LANES, LANES)] = pay[s, mid, :].astype(F32)
                return 0

            lax.fori_loop(0, 3, body, 0)
            part = pl.ds(3 * a * chans, 3 * chans)
            out.append(move(full.at[part], dst.at[part], osem.at[3 + 3 * n + a]))

    kernel(0, b2, get_2, f2, k2o)

    get_v.wait()
    sums = jnp.sum(bv[...], axis=0)
    for ref, k in ((g1, 0), (s1, 1), (o1, 2), (g2, 3), (s2, 4), (o2, 5), (g3, 6), (s3, 7), (ooo, 8)):
        ref[...] = sums[k]
    for ref, k in ((eoo, 9), (oio, 13)):
        ref[pl.ds(0, chans)] = sums[k]
        ref[pl.ds(chans, chans)] = sums[k + 1]
    for a in range(2):
        for b in range(2):
            fe[pl.ds(a * chans, chans), pl.ds(b * chans, chans)] = lax.dot_general(
                bv[:, 11 + a, :], bv[:, 9 + b, :], (((0,), (0,)), ((), ())),
                preferred_element_type=F32, precision=lax.Precision.HIGHEST,
            )
    out.append(move(fe, ewo, osem.at[2]))

    kernel(1, b1, get_1, f1, k1o)
    for k, dst in enumerate((res_o, ing_o)):
        get_r[k].wait()
        out.append(move(br.at[k], dst, osem.at[k]))

    get_p.wait()
    low = lax.broadcasted_iota(jnp.int32, (1, LANES), 1) < HEAD_DIM
    pairs = 3 * heads // 2
    odd = (3 * heads) % 2
    sides = []
    for s in range(2):
        blocks = [bp[s, pl.ds(k * chans, chans), :].astype(F32) for k in range(pairs)]
        if odd:
            last = bp[s, pl.ds(pairs * chans, chans // 2), :].astype(F32)
            blocks.append(jnp.concatenate([last, pltpu.roll(last, HEAD_DIM, 1)], axis=0))
        sides.append(blocks)
    cols = sides[0] + sides[1]
    if odd:
        turned = [pltpu.roll(b, HEAD_DIM, 1) for b in sides[1]]
        cols = sides[0][:-1] + [jnp.where(low, sides[0][-1], turned[0])]
        cols += [jnp.where(low, turned[k], turned[k + 1]) for k in range(pairs)]
    for k, b in enumerate(cols):
        fi[:, pl.ds(k * LANES, LANES)] = b
    out.append(move(fi, pio, osem.at[9]))
    base = pairs * chans + odd * (chans // 2)
    for s in range(2):
        for b in range(chans // LANES):
            fo[pl.ds(s * own, own), pl.ds(b * LANES, LANES)] = bp[s, pl.ds(base + b * own, own), :].astype(F32)
    out.append(move(fo, poo, osem.at[10]))
    for cp in out:
        cp.wait()


def time_features(timesteps, width):
    half_width = width // 2
    frequency = jnp.exp(-math.log(10000.0) * jnp.arange(half_width, dtype=jnp.float32) / half_width)
    angles = timesteps.astype(jnp.float32)[:, None] * frequency[None, :]
    return jnp.concatenate([jnp.cos(angles), jnp.sin(angles)], axis=1)


def local(
    n_img,
    images_in, extents, timesteps, gain_first, shift_first, kernel_first, offset_first, embed_weight, embed_offset,
    gain_second, shift_second, kernel_second, offset_second, gain_attend, shift_attend, project_in, offset_in,
    project_out, offset_out, out_grad,
):
    _, stripe_rows, side, chans = images_in.shape
    px = side * side
    half = stripe_rows * side
    te = embed_weight.shape[0]
    own = chans // 2
    heads = own // HEAD_DIM
    taps = 9
    unit = 16 * n_img
    real_k = taps * (chans + chans // 2)
    real_p = 3 * heads * HEAD_DIM * chans // LANES + own * (chans // LANES)
    rows_k = cdiv(real_k, unit) * unit
    rows_p = cdiv(real_p, unit) * unit
    bits = []
    while 2 ** len(bits) < n_img:
        bits.append(2 ** len(bits))
    nbits = len(bits)

    t_act = jax.nn.silu(time_features(timesteps, te))
    vm = pl.BlockSpec(memory_space=pltpu.VMEM)
    anym = pl.BlockSpec(memory_space=pl.ANY)
    smem = pl.BlockSpec(memory_space=pltpu.SMEM)
    sds = jax.ShapeDtypeStruct
    V = pltpu.VMEM
    padded = px + 2 * side
    wide = 3 * heads * LANES
    flow_sems = 2 * nbits + 2
    n_sem = (2 * len(KERNEL_FLOWS) + len(PROJECT_FLOWS)) * flow_sems + nbits
    scratch = [
        V((taps * chans, chans), BF), V((taps * chans, chans), BF),
        V((chans + WIN - own, chans), BF), V((te, 2 * chans), BF), V((chans, wide), BF),
        V((px, WIN), BF), V((px, chans), BF), V((px, LANES), F32), V((1, 2 * chans), F32),
        V((2, padded, WIN), BF), V((2, padded, WIN), BF), V((2, px, WIN), BF), V((2, padded, WIN), BF), V((2, padded, WIN), BF),
        V((px, WIN), F32), V((px, WIN), F32), V((px, WIN), F32), V((px, WIN), F32),
        V((heads, px, LANES), BF), V((heads, px, LANES), BF), V((heads, px, LANES), BF),
        V((heads, LANES, px), BF), V((heads, LANES, px), BF), V((heads, LANES, px), BF), V((WIN, px), BF), V((px, wide), BF),
        V((px, chans), F32), V((half, chans), F32), V((px, WIN), BF), V((px, WIN), BF),
        V((3, padded, WIN), BF), V((chans, px), BF), V((chans, px), BF), V((chans, px), BF), V((half, WIN), BF), V((half, chans), F32),
        V((rows_k, LANES), BF), V((rows_k, LANES), BF), V((rows_p, LANES), BF),
        V((rows_k, LANES), BF), V((rows_k, LANES), BF), V((rows_p, LANES), BF),
        V((2, rows_k, LANES), BF), V((2, rows_k, LANES), BF), V((2, rows_p, LANES), BF),
        V((16, chans), F32), V((16, chans), F32), V((n_img, 16, chans), F32),
        pltpu.SemaphoreType.DMA((7,)), pltpu.SemaphoreType.DMA((16,)), pltpu.SemaphoreType.DMA((11,)), pltpu.SemaphoreType.DMA((11,)),
        pltpu.SemaphoreType.DMA((n_sem,)), pltpu.SemaphoreType.DMA((n_sem,)),
    ]
    res, ing, pk1, pk2, pp, vec = pl.pallas_call(
        functools.partial(block_kernel, (side, chans, n_img, real_k, real_p, tuple(bits), flow_sems)),
        out_shape=(
            sds((half, chans), BF), sds((half, chans), BF), sds((2, rows_k, LANES), BF), sds((2, rows_k, LANES), BF),
            sds((2, rows_p, LANES), BF), sds((n_img, 16, chans), F32),
        ),
        in_specs=[anym, anym, smem] + [vm] * 12 + [anym, anym, anym, anym, anym],
        out_specs=(vm, vm, anym, anym, anym, anym),
        scratch_shapes=scratch,
        compiler_params=pltpu.CompilerParams(collective_id=0, has_side_effects=True, vmem_limit_bytes=60 * 2**20),
        cost_estimate=pl.CostEstimate(flops=2 * 10**10, bytes_accessed=2 * 10**7, transcendentals=4 * 10**6),
        name="block",
    )(
        images_in.reshape(half, chans), out_grad.reshape(half, chans), extents, gain_first, shift_first, offset_first,
        gain_second, shift_second, offset_second, gain_attend, shift_attend, offset_out, t_act, embed_offset, offset_in,
        kernel_first.reshape(taps * chans, chans), kernel_second.reshape(taps * chans, chans),
        project_in, project_out, embed_weight,
    )

    row = sds((chans,), F32)
    row2 = sds((2 * chans,), F32)
    kern = sds((taps * chans, chans), F32)
    stripe = sds((half, chans), BF)
    outs = pl.pallas_call(
        functools.partial(finish_kernel, (chans, heads)),
        out_shape=(
            stripe, stripe, row, row, kern, row, sds((te, 2 * chans), F32), row2, row, row, kern, row, row, row,
            sds((chans, 3 * chans), F32), row2, sds((chans, chans), F32), row,
        ),
        in_specs=[anym] * 6,
        out_specs=(anym, anym, vm, vm, anym, vm, anym, vm, vm, vm, anym, vm, vm, vm, anym, vm, anym, vm),
        scratch_shapes=[
            V((2, rows_k, LANES), BF), V((2, rows_k, LANES), BF), V((2, rows_p, LANES), BF), V((n_img, 16, chans), F32),
            V((2, half, chans), BF), V((taps * chans, chans), F32), V((taps * chans, chans), F32), V((te, 2 * chans), F32),
            V((chans, 3 * chans), F32), V((chans, chans), F32),
            pltpu.SemaphoreType.DMA((10,)), pltpu.SemaphoreType.DMA((11,)),
        ],
        compiler_params=pltpu.CompilerParams(vmem_limit_bytes=60 * 2**20),
        cost_estimate=pl.CostEstimate(flops=10**8, bytes_accessed=23 * 10**6, transcendentals=0),
        name="finish",
    )(pk1, pk2, pp, vec, res, ing)
    res, ing, *outs = outs
    shapes = (
        gain_first, shift_first, kernel_first, offset_first, embed_weight, embed_offset, gain_second, shift_second,
        kernel_second, offset_second, gain_attend, shift_attend, project_in, offset_in, project_out, offset_out,
    )
    outs = [o.reshape(s.shape) for o, s in zip(outs, shapes)]
    return (res.reshape(images_in.shape), ing.reshape(images_in.shape), *outs)


def solution(mesh):
    n_img = mesh.shape["img"]
    stripe = P("img", "pix", None, None)
    in_specs = (stripe, P("img", None), P("img")) + (P(),) * 16 + (stripe,)
    out_specs = (stripe, stripe) + (P(),) * 16
    return jax.shard_map(
        functools.partial(local, n_img), mesh=mesh, in_specs=in_specs, out_specs=out_specs, check_vma=False
    )
```

time: 154 us -> 121 us (0.79)
  Pallas kernels: 150 us -> 119 us
    pallas_call x1, Pallas kernels: 139 us -> 111 us  [local(): pl.pallas_call(functools.partial(block_kernel, (side, chans, n_img, real_...]
    pallas_call x1, Pallas kernels: 11.3 us -> 8.58 us  [local(): pl.pallas_call(functools.partial(finish_kernel, (chans, heads)), out_shap...]
where the time goes in v2:
time: 121 us
  Pallas kernels  119 us (98%)
  between operations  1.49 us (1%)
    pallas_call x1, Pallas kernels, local(): pl.pallas_call(functools.partial(block_kernel, (side, chans, n_img, real_...  111 us
    pallas_call x1, Pallas kernels, local(): pl.pallas_call(functools.partial(finish_kernel, (chans, heads)), out_shap...  8.58 us

profile of v2, /device:TPU:0, one launch (start us, length us, event | category | flops | bytes accessed | tf_op | source)
XLA Modules:
  0.0 121.3 jit_solution(5475355557367225518)
XLA Ops:
  1.4 0.6 divide_multiply_fusion.refs_12_
  2.0 110.5 %block.1 = (bf16[512,384]{1,0:T(8,128)(2,1)}, bf16[512,384]{1,0:T(8,128)(2,1)}, bf16[2,5376,128]{2,1,0:T(8,128)(2,1)}, bf16[2,5376,128]{2,1,0:T(8,128)(2,1)}, bf...) custom-call(bf16[512,384]{1,0:T(8,128)(2,1)} %bitcast.13, bf16[512,384]{1,0:T(8,128)(2,1)} %bitcast.14, ...), custom_call_target="tpu_custom_call" | custom-call | flops 20000000000 | bytes 20000000 | tf_op jit(solution)/shard_map/block/pallas_call | solution.py:983
  112.5 8.6 %finish.1 = (bf16[512,384]{1,0:T(8,128)(2,1)}, bf16[512,384]{1,0:T(8,128)(2,1)}, f32[384]{0:T(512)}, f32[384]{0:T(512)}, f32[3456,384]{1,0:T(8,128)}, /*index=5*...) custom-call(bf16[2,5376,128]{2,1,0:T(8,128)(2,1)} %get-tuple-element, ...), custom_call_target="tpu_custom_call" | custom-call | flops 100000000 | bytes 23000000 | tf_op jit(solution)/shard_map/finish/pallas_call | solution.py:1006
  (3 shorter events, 0.1 us)

commit v3 on v2

--- a/solution.py
+++ b/solution.py
@@ -17,25 +17,23 @@
 MESH = pl.DeviceIdType.MESH
 WIN = 256
 LANES = 128
-RC = 128
+RC = 256
 MC = 512
 TC = 256
-KERNEL_FLOWS = ((0, 4), (1, 4), (2, 3), (0, 4), (1, 3), (2, 3))
-PROJECT_FLOWS = ((0, 3), (1, 3), (2, 3))
+X_FIRST, Y_FIRST, Z_FIRST = (0, 1, 2, 3), (1, 2, 0, 3), (2, 0, 1, 3)
+KERNEL_FLOWS = ((X_FIRST, 4), (Y_FIRST, 4), (Z_FIRST, 4), (X_FIRST, 3), (Y_FIRST, 3), (Z_FIRST, 3))
+PROJECT_FLOWS = ((X_FIRST, 3), (Y_FIRST, 3), (Z_FIRST, 3))
+SECOND, FIRST, PROJECT = tuple(range(16)), tuple(range(16, 32)), tuple(range(32, 48))
 PLAN = (
-    (0,),
-    (2, 1),
-    (3, 4, 5, 0),
-    (2, 1),
-    (4, 3, 5, 0),
-    (13, 12),
-    (2, 14, 1),
-    (8, 6, 7, 4, 5, 3, 0, 12),
-    (13, 2, 9, 10, 1, 14, 11, 8, 6, 7),
-    (4, 5, 12),
-    (3, 13, 0, 10, 9, 11, 14, 6, 2, 7, 8, 1),
-    (4, 5, 10, 12, 11, 0, 2, 9, 1, 3, 4, 13, 5, 14, 6, 0, 7, 2, 8, 10, 1, 12, 3, 5, 11, 9, 4, 13, 14, 6, 0, 7, 8, 2, 13)
-    + (10, 1, 11, 12, 3, 9, 7, 5, 10, 4, 14, 6, 8, 11, 13, 9, 12, 3, 7, 14, 6, 10, 8, 11, 13, 9, 12, 14, 8, 7, 6, 11, 10, 9),
+    (),
+    SECOND,
+    (),
+    SECOND,
+    SECOND + PROJECT,
+    SECOND + FIRST + PROJECT,
+    (),
+    SECOND + FIRST + PROJECT,
+    (),
 )
 
 
@@ -187,12 +185,12 @@
     side, chans, n_img, real_k, real_p, bits, flow_sems = dims
     (
         x_in, g_in, ext, p_g1, p_s1, p_o1, p_g2, p_s2, p_o2, p_g3, p_s3, p_oo, t_act, e_off, off_in, k1_h, k2_h, wi_h, wo_h, ew_h,
-        res_out, ing_out, pk1_o, pk2_o, pp_o, vec_o,
+        res_v, ing_v, out1, out2, outp, vall,
         k1, k2, wo, ew, wq, xw, gf, mask, film, act1, act2, act3, dd2, dd1,
         cv, hid, tmp, resid, qa, ka, va, kat, vat, dot_t, att_t, dqkv,
-        tsum, trecv, datt_s, datt_r, dm, act_t1, act_t2, act_t3, ing_r, tsum_i,
-        pay1, pay2, payp, rb1, rb2, rbp, out1, out2, outp, vx, vr, vall,
-        lsem, os, xs, xr, fs, fr,
+        tsum, trecv, datt_s, datt_r, dm, act_t1, act_t2, act_t3, ing_r,
+        pay1, pay2, payp, rb1, rb2, rbp, vx, vr,
+        lsem, xs, xr, fs, fr,
     ) = refs
     img = lax.axis_index("img")
     c = lax.axis_index("pix")
@@ -218,10 +216,11 @@
 
     barrier = pltpu.get_barrier_semaphore()
     peers = [(img, oc)]
-    turns = []
-    for r in range(3):
-        near = list(bits[:3])[r:] + list(bits[:3])[:r]
-        turns.append([[bit] for bit in near + list(bits[3:])])
+
+    def stages(order):
+        near = [bits[k] for k in order if k < nbits]
+        return [[bit] for bit in near + list(bits[len(order) :])]
+
     for bit in bits:
         peers.append((xor(img, [bit], 1), c))
     for peer in peers:
@@ -264,7 +263,7 @@
     inv_entries = 1.0 / jnp.full((1, WIN), rows_e * cols_e * per, jnp.int32).astype(F32)
     gi = lax.broadcasted_iota(jnp.int32, (WIN, WIN), 0) + LANES * c
     gj = lax.broadcasted_iota(jnp.int32, (WIN, WIN), 1) + LANES * c
-    same = (gi // per == gj // per).astype(F32)
+    same = (gi // per == gj // per).astype(F32).astype(BF)
 
     def pvec(ref):
         return ref[win].reshape(1, WIN)
@@ -274,8 +273,14 @@
     gain3, shift3 = pvec(p_g3), pvec(p_s3)
 
     def group_totals(a, b):
-        both = dot_hi(jnp.concatenate([a, b], axis=0), same)
-        return jnp.sum(both[:8], axis=0, keepdims=True), jnp.sum(both[8:], axis=0, keepdims=True)
+        both = jnp.concatenate([a, b], axis=0)
+        high = both.astype(BF)
+        rest = both - high.astype(F32)
+        mid = rest.astype(BF)
+        low = (rest - mid.astype(F32)).astype(BF)
+        o = dot(jnp.concatenate([high, mid, low], axis=0), same)
+        o = o[:16] + o[16:32] + o[32:]
+        return jnp.sum(o[:8], axis=0, keepdims=True), jnp.sum(o[8:], axis=0, keepdims=True)
 
     def total(a):
         return jnp.sum(a, axis=0, keepdims=True)
@@ -512,7 +517,7 @@
             dqkv[:, pl.ds(aligned((3 * h + k) * LANES, LANES), LANES)] = jnp.where(low1, d, 0.0).astype(BF)
         return 0
 
-    lax.fori_loop(0, heads, body, 0)
+    lax.fori_loop(0, heads, body, 0, unroll=True)
 
     def body(j, _):
         at = rows_at(j, MC)
@@ -533,10 +538,9 @@
     used = [0]
     flows = {}
 
-    def flow_of(key, pay, rbuf, gathered, dst, k, base, size):
+    def flow_of(key, pay, rbuf, gathered, order, base, size):
         if size:
-            flow = Flow(pay, rbuf, gathered, base, size, turns[k], (fs, fr, used[0]), c, img)
-            flow.dst = dst
+            flow = Flow(pay, rbuf, gathered, base, size, stages(order), (fs, fr, used[0]), c, img)
             used[0] += flow_sems
             flows[key] = flow
             flow.advance()
@@ -546,19 +550,10 @@
             if key in flows:
                 flows[key].advance()
 
-    stores = []
-
-    def store(src, dst):
-        cp = pltpu.make_async_copy(src, dst, os.at[len(stores)])
-        cp.start()
-        stores.append(cp)
-
     def hand_out(key):
         flow = flows.pop(key)
         for cp in flow.forwards:
             cp.wait()
-        at = pl.ds(flow.base, flow.rows)
-        store(flow.out.at[:, at], flow.dst.at[:, at])
 
     swap_da.wait()
 
@@ -593,63 +588,65 @@
     vx[pl.ds(5, 1), win] = total(lax.fori_loop(0, px // RC, body, zero8))
     swap_d2 = swap(dd2.at[c, inner], dd2.at[c, inner], 7)
 
-    def body(j, _):
-        tmp[rows_at(j, MC), :] = conv(dd2, c, k2, True, j)
-        return 0
-
-    lax.fori_loop(0, px // MC, body, 0)
-    swap_d2.wait()
-
-    def shifted(dd):
+    own_lanes = pl.ds(aligned(LANES * c, LANES), LANES)
+    mid_lanes = pl.ds(aligned(LANES * oc, LANES), LANES)
+    hc = chans // 2
+    my_half = pl.ds(aligned(hc * c, HEAD_DIM), hc)
+
+    def shift_into(first_lane, read):
+        lanes = pl.ds(first_lane, LANES)
+
         def body(j, _):
-            d = dd[c, pad_at(j, TC), :].astype(F32)
-            mid = dd[oc, pad_at(j, TC), pl.ds(aligned(LANES * c, LANES), LANES)].astype(F32)
-            none = jnp.zeros((TC, LANES), F32)
-            d = d + jnp.where(first, jnp.concatenate([none, mid], axis=1), jnp.concatenate([mid, none], axis=1))
             at = pad_at(j, TC)
-            dm[0, at, :] = (pltpu.roll(d, TC - 1, 0) * not_last[:TC]).astype(BF)
-            dm[1, at, :] = d.astype(BF)
-            dm[2, at, :] = (pltpu.roll(d, 1, 0) * not_first[:TC]).astype(BF)
+            d = read(at)
+            dm[0, at, lanes] = (pltpu.roll(d, TC - 1, 0) * not_last[:TC, :LANES]).astype(BF)
+            dm[1, at, lanes] = d.astype(BF)
+            dm[2, at, lanes] = (pltpu.roll(d, 1, 0) * not_first[:TC, :LANES]).astype(BF)
             return 0
 
         lax.fori_loop(0, px // TC, body, 0)
 
-    def kernel_grad(act_t, key, pay, rbuf, gathered, dst, points):
-        hc = chans // 2
+    def kernel_grad(act_t, dd, wait, key, pay, rbuf, gathered, point):
         unit = 16 * n_img
-
-        def body(tap, _):
-            a = tap // 3
-            b = tap % 3
-            o = dot(act_t[...], dm[b, pl.ds(aligned(side * (2 - a), 32), px), :])
-            lo, hi = o[:, :LANES], o[:, LANES:]
-            main = jnp.where(first, lo, hi)
-            mid = jnp.where(first, hi[:hc], lo[hc:])
-            at = tap * (chans + hc)
-            pay[pl.ds(aligned(at, HEAD_DIM), chans), :] = main.astype(BF)
-            pay[pl.ds(aligned(at + chans, HEAD_DIM), hc), :] = mid.astype(BF)
-            return 0
-
-        done = 0
-        base = 0
-        for k, units in enumerate(shares(pay.shape[0] // unit, KERNEL_FLOWS)):
-            need = min(9, cdiv(base + units * unit, chans + hc))
-            if need > done:
-                lax.fori_loop(done, need, body, 0)
-                done = need
-            flow_of(key + k, pay, rbuf, gathered, dst, KERNEL_FLOWS[k][0], base, units * unit)
-            base += units * unit
-            if k in points:
-                advance(points[k])
-
-    shifted(dd2)
-    kernel_grad(act_t2, 0, pay2, rb2, out2, pk2_o, {})
+        sizes = [units * unit for units in shares(pay.shape[0] // unit, KERNEL_FLOWS)]
+        begun = []
+
+        def begin(rows):
+            while len(begun) < len(sizes) and sum(sizes[: len(begun) + 1]) <= rows:
+                k = len(begun)
+                flow_of(key + k, pay, rbuf, gathered, KERNEL_FLOWS[k][0], sum(sizes[:k]), sizes[k])
+                begun.append(k)
+
+        def tap_rows(tap, lanes):
+            return dm[tap % 3, pl.ds(side * (2 - tap // 3), px), lanes]
+
+        def block(rows, base, lanes):
+            n = rows.shape[0]
+            for tap in range(0, 9, 2):
+                if tap < 8:
+                    o = dot(rows[...], jnp.concatenate([tap_rows(tap, lanes), tap_rows(tap + 1, lanes)], axis=1))
+                    pay[pl.ds(base + tap * n, n), :] = o[:, :LANES].astype(BF)
+                    pay[pl.ds(base + (tap + 1) * n, n), :] = o[:, LANES:].astype(BF)
+                else:
+                    pay[pl.ds(base + tap * n, n), :] = dot(rows[...], tap_rows(tap, lanes)).astype(BF)
+                begin(base + min(tap + 2, 9) * n)
+
+        shift_into(0, lambda at: dd[c, at, own_lanes].astype(F32))
+        block(act_t, 0, pl.ds(0, LANES))
+        if point is not None:
+            advance(point)
+        wait()
+        shift_into(LANES, lambda at: dd[c, at, mid_lanes].astype(F32) + dd[oc, at, own_lanes].astype(F32))
+        block(act_t.at[my_half], 9 * chans, pl.ds(LANES, LANES))
+        begin(pay.shape[0])
+
+    kernel_grad(act_t2, dd2, swap_d2.wait, SECOND[0], pay2, rb2, out2, None)
 
     def body(j, carry):
         at = rows_at(j, MC)
         pre = cv[at, :] * mul2 + add2
         sg = sigmoid(pre)
-        u = (tmp[at, :] + conv(dd2, oc, k2, True, j)) * (sg * (1.0 + pre * (1.0 - sg)))
+        u = (conv(dd2, c, k2, True, j) + conv(dd2, oc, k2, True, j)) * (sg * (1.0 + pre * (1.0 - sg)))
         tmp[at, :] = u
         return back_sums(carry, u, (cv[at, :] - mean2) * rstd2)
 
@@ -675,6 +672,9 @@
     swap_d1 = swap(dd1.at[c, inner], dd1.at[c, inner], 8)
 
     advance(1)
+
+    kernel_grad(act_t1, dd1, swap_d1.wait, FIRST[0], pay1, rb1, out1, 2)
+    advance(3)
 
     for k in range(3 * heads // 2):
         o = dot(act_t3[...], dqkv[:, pl.ds(2 * LANES * k, 2 * LANES)])
@@ -704,35 +704,23 @@
         vx[pl.ds(13, 1), pl.ds(LANES * h, LANES)] = jnp.where(first, sums, 0.0)
         vx[pl.ds(14, 1), pl.ds(LANES * h, LANES)] = jnp.where(first, 0.0, sums)
 
-    advance(2)
+    advance(4)
     at = 0
     for k, units in enumerate(shares(payp.shape[0] // (16 * n_img), PROJECT_FLOWS)):
-        flow_of(12 + k, payp, rbp, outp, pp_o, PROJECT_FLOWS[k][0], at, units * 16 * n_img)
+        flow_of(PROJECT[0] + k, payp, rbp, outp, PROJECT_FLOWS[k][0], at, units * 16 * n_img)
         at += units * 16 * n_img
-
-    swap_d1.wait()
-    shifted(dd1)
-    advance(3)
-    kernel_grad(act_t1, 6, pay1, rb1, out1, pk1_o, {2: 4, 3: 5, 4: 6})
-
-    def body(j, _):
-        tmp[rows_at(j, MC), :] = conv(dd1, c, k1, True, j)
-        return 0
-
-    lax.fori_loop(0, px // MC, body, 0)
-    advance(7)
 
     def body(j, carry):
         at = rows_at(j, MC)
         x = xw[at, :].astype(F32)
         pre = x * mul1 + add1
         sg = sigmoid(pre)
-        u = (tmp[at, :] + conv(dd1, oc, k1, True, j)) * (sg * (1.0 + pre * (1.0 - sg)))
+        u = (conv(dd1, c, k1, True, j) + conv(dd1, oc, k1, True, j)) * (sg * (1.0 + pre * (1.0 - sg)))
         tmp[at, :] = u
         return back_sums(carry, u, (x - mean1) * rstd1)
 
     s0, s1 = lax.fori_loop(0, px // MC, body, (zero8, zero8))
-    advance(8)
+    advance(5)
     vx[pl.ds(0, 1), win] = total(s1) * own_f
     vx[pl.ds(1, 1), win] = total(s0) * own_f
 
@@ -787,7 +775,7 @@
 
     vectors = Gather()
     vectors.advance()
-    advance(9)
+    advance(6)
 
     def body(j, _):
         at = rows_at(j, TC)
@@ -798,18 +786,19 @@
     lax.fori_loop(0, px // TC, body, 0)
     swap_t = swap(tsum.at[other_rows], trecv, 6)
 
-    advance(10)
+    advance(7)
     vectors.advance()
 
+    swap_t.wait()
+    res_v[...] = (tsum[my_rows, :] + trecv[...] + p_oo[...].reshape(1, -1)).astype(BF)
     swap_i.wait()
-    tsum_i[...] = jnp.zeros((half, chans), F32)
-    tsum_i[:, win] = tmp[my_rows, :]
-    tsum_i[:, owin] += ing_r[...].astype(F32)
-    ing_out[...] = tsum_i[...].astype(BF)
-    swap_t.wait()
-    res_out[...] = (tsum[my_rows, :] + trecv[...] + p_oo[...].reshape(1, -1)).astype(BF)
+    top_rows = pl.ds(0, half)
+    tsum[top_rows, :] = jnp.zeros((half, chans), F32)
+    tsum[top_rows, win] = tmp[my_rows, :]
+    tsum[top_rows, owin] += ing_r[...].astype(F32)
+    ing_v[...] = tsum[top_rows, :].astype(BF)
     ended = {}
-    for n, key in enumerate(PLAN[11]):
+    for n, key in enumerate(PLAN[8]):
         if key in flows:
             flows[key].advance()
             if flows[key].ended():
@@ -824,17 +813,14 @@
         vectors.advance()
     while vectors.copies:
         vectors.advance()
-    store(vall, vec_o)
     for key in sorted(flows, key=lambda k: ended.get(k, 0)):
         hand_out(key)
-    for cp in stores:
-        cp.wait()
-
-
-def finish_kernel(dims, pk1, pk2, pp, vec, res, ing, *refs):
+
+
+def finish_kernel(dims, b1, b2, bp, bv, res, ing, *refs):
     chans, heads = dims
     (res_o, ing_o, g1, s1, k1o, o1, ewo, eoo, g2, s2, k2o, o2, g3, s3, pio, oio, poo, ooo) = refs[:18]
-    (b1, b2, bp, bv, br, f1, f2, fe, fi, fo, isem, osem) = refs[18:]
+    (f1, f2, fe, fi, fo, fw, fv, osem) = refs[18:]
     hc = chans // 2
     own = chans // 2
     te = fe.shape[0]
@@ -844,26 +830,17 @@
         cp.start()
         return cp
 
-    each = 3 * (chans + hc)
-    get_2 = [move(pk2.at[:, pl.ds(a * each, each)], b2.at[:, pl.ds(a * each, each)], isem.at[a]) for a in range(3)]
-    get_v = move(vec, bv, isem.at[3])
-    get_1 = [move(pk1.at[:, pl.ds(a * each, each)], b1.at[:, pl.ds(a * each, each)], isem.at[4 + a]) for a in range(3)]
-    get_p = move(pp, bp, isem.at[7])
-    get_r = [move(src, br.at[k], isem.at[8 + k]) for k, src in enumerate((res, ing))]
-    out = []
-
-    def kernel(n, pay, get, full, dst):
+    out = [move(res, res_o, osem.at[0]), move(ing, ing_o, osem.at[1])]
+
+    def kernel(n, pay, full, dst):
         for a in range(3):
-            get[a].wait()
 
             def body(b, _, a=a):
                 tap = 3 * a + b
-                src = tap * (chans + hc)
-                at = pl.ds(pl.multiple_of(tap * chans, LANES), chans)
-                main = pl.ds(pl.multiple_of(src, HEAD_DIM), chans)
+                at = main = pl.ds(pl.multiple_of(tap * chans, LANES), chans)
                 full[at, pl.ds(0, LANES)] = pay[0, main, :].astype(F32)
                 full[at, pl.ds(2 * LANES, LANES)] = pay[1, main, :].astype(F32)
-                mid = pl.ds(pl.multiple_of(src + chans, HEAD_DIM), hc)
+                mid = pl.ds(pl.multiple_of(9 * chans + tap * hc, HEAD_DIM), hc)
                 for s in range(2):
                     to = pl.ds(pl.multiple_of(tap * chans + s * hc, HEAD_DIM), hc)
                     full[to, pl.ds(LANES, LANES)] = pay[s, mid, :].astype(F32)
@@ -873,15 +850,18 @@
             part = pl.ds(3 * a * chans, 3 * chans)
             out.append(move(full.at[part], dst.at[part], osem.at[3 + 3 * n + a]))
 
-    kernel(0, b2, get_2, f2, k2o)
-
-    get_v.wait()
+    kernel(0, b2, f2, k2o)
+
     sums = jnp.sum(bv[...], axis=0)
-    for ref, k in ((g1, 0), (s1, 1), (o1, 2), (g2, 3), (s2, 4), (o2, 5), (g3, 6), (s3, 7), (ooo, 8)):
-        ref[...] = sums[k]
-    for ref, k in ((eoo, 9), (oio, 13)):
-        ref[pl.ds(0, chans)] = sums[k]
-        ref[pl.ds(chans, chans)] = sums[k + 1]
+    for n, (dst, k) in enumerate(((g1, 0), (s1, 1), (o1, 2), (g2, 3), (s2, 4), (o2, 5), (g3, 6), (s3, 7), (ooo, 8))):
+        at = pl.ds(n * chans, chans)
+        fv[at] = sums[k]
+        out.append(move(fv.at[at], dst, osem.at[11 + n]))
+    for n, (dst, k) in enumerate(((eoo, 9), (oio, 13))):
+        at = pl.ds(2 * n * chans, 2 * chans)
+        fw[pl.ds(2 * n * chans, chans)] = sums[k]
+        fw[pl.ds((2 * n + 1) * chans, chans)] = sums[k + 1]
+        out.append(move(fw.at[at], dst, osem.at[20 + n]))
     for a in range(2):
         for b in range(2):
             fe[pl.ds(a * chans, chans), pl.ds(b * chans, chans)] = lax.dot_general(
@@ -890,12 +870,8 @@
             )
     out.append(move(fe, ewo, osem.at[2]))
 
-    kernel(1, b1, get_1, f1, k1o)
-    for k, dst in enumerate((res_o, ing_o)):
-        get_r[k].wait()
-        out.append(move(br.at[k], dst, osem.at[k]))
-
-    get_p.wait()
+    kernel(1, b1, f1, k1o)
+
     low = lax.broadcasted_iota(jnp.int32, (1, LANES), 1) < HEAD_DIM
     pairs = 3 * heads // 2
     odd = (3 * heads) % 2
@@ -972,24 +948,23 @@
         V((heads, px, LANES), BF), V((heads, px, LANES), BF), V((heads, px, LANES), BF),
         V((heads, LANES, px), BF), V((heads, LANES, px), BF), V((heads, LANES, px), BF), V((WIN, px), BF), V((px, wide), BF),
         V((px, chans), F32), V((half, chans), F32), V((px, WIN), BF), V((px, WIN), BF),
-        V((3, padded, WIN), BF), V((chans, px), BF), V((chans, px), BF), V((chans, px), BF), V((half, WIN), BF), V((half, chans), F32),
+        V((3, padded, WIN), BF), V((chans, px), BF), V((chans, px), BF), V((chans, px), BF), V((half, WIN), BF),
         V((rows_k, LANES), BF), V((rows_k, LANES), BF), V((rows_p, LANES), BF),
         V((rows_k, LANES), BF), V((rows_k, LANES), BF), V((rows_p, LANES), BF),
-        V((2, rows_k, LANES), BF), V((2, rows_k, LANES), BF), V((2, rows_p, LANES), BF),
-        V((16, chans), F32), V((16, chans), F32), V((n_img, 16, chans), F32),
-        pltpu.SemaphoreType.DMA((7,)), pltpu.SemaphoreType.DMA((16,)), pltpu.SemaphoreType.DMA((11,)), pltpu.SemaphoreType.DMA((11,)),
+        V((16, chans), F32), V((16, chans), F32),
+        pltpu.SemaphoreType.DMA((7,)), pltpu.SemaphoreType.DMA((11,)), pltpu.SemaphoreType.DMA((11,)),
         pltpu.SemaphoreType.DMA((n_sem,)), pltpu.SemaphoreType.DMA((n_sem,)),
     ]
     res, ing, pk1, pk2, pp, vec = pl.pallas_call(
         functools.partial(block_kernel, (side, chans, n_img, real_k, real_p, tuple(bits), flow_sems)),
         out_shape=(
-            sds((half, chans), BF), sds((half, chans), BF), sds((2, rows_k, LANES), BF), sds((2, rows_k, LANES), BF),
-            sds((2, rows_p, LANES), BF), sds((n_img, 16, chans), F32),
+            V((half, chans), BF), V((half, chans), BF), V((2, rows_k, LANES), BF), V((2, rows_k, LANES), BF),
+            V((2, rows_p, LANES), BF), V((n_img, 16, chans), F32),
         ),
         in_specs=[anym, anym, smem] + [vm] * 12 + [anym, anym, anym, anym, anym],
-        out_specs=(vm, vm, anym, anym, anym, anym),
+        out_specs=(vm,) * 6,
         scratch_shapes=scratch,
-        compiler_params=pltpu.CompilerParams(collective_id=0, has_side_effects=True, vmem_limit_bytes=60 * 2**20),
+        compiler_params=pltpu.CompilerParams(collective_id=0, has_side_effects=True, vmem_limit_bytes=50 * 2**20),
         cost_estimate=pl.CostEstimate(flops=2 * 10**10, bytes_accessed=2 * 10**7, transcendentals=4 * 10**6),
         name="block",
     )(
@@ -1009,18 +984,17 @@
             stripe, stripe, row, row, kern, row, sds((te, 2 * chans), F32), row2, row, row, kern, row, row, row,
             sds((chans, 3 * chans), F32), row2, sds((chans, chans), F32), row,
         ),
-        in_specs=[anym] * 6,
-        out_specs=(anym, anym, vm, vm, anym, vm, anym, vm, vm, vm, anym, vm, vm, vm, anym, vm, anym, vm),
+        in_specs=[vm] * 6,
+        out_specs=(anym,) * 18,
         scratch_shapes=[
-            V((2, rows_k, LANES), BF), V((2, rows_k, LANES), BF), V((2, rows_p, LANES), BF), V((n_img, 16, chans), F32),
-            V((2, half, chans), BF), V((taps * chans, chans), F32), V((taps * chans, chans), F32), V((te, 2 * chans), F32),
-            V((chans, 3 * chans), F32), V((chans, chans), F32),
-            pltpu.SemaphoreType.DMA((10,)), pltpu.SemaphoreType.DMA((11,)),
+            V((taps * chans, chans), F32), V((taps * chans, chans), F32), V((te, 2 * chans), F32),
+            V((chans, 3 * chans), F32), V((chans, chans), F32), V((4 * chans,), F32), V((9 * chans,), F32),
+            pltpu.SemaphoreType.DMA((22,)),
         ],
-        compiler_params=pltpu.CompilerParams(vmem_limit_bytes=60 * 2**20),
+        compiler_params=pltpu.CompilerParams(vmem_limit_bytes=32 * 2**20),
         cost_estimate=pl.CostEstimate(flops=10**8, bytes_accessed=23 * 10**6, transcendentals=0),
         name="finish",
-    )(pk1, pk2, pp, vec, res, ing)
+    )(*(pltpu.with_memory_space_constraint(x, pltpu.VMEM) for x in (pk1, pk2, pp, vec, res, ing)))
     res, ing, *outs = outs
     shapes = (
         gain_first, shift_first, kernel_first, offset_first, embed_weight, embed_offset, gain_second, shift_second,

time: 121 us -> 114 us (0.942)
  Pallas kernels: 119 us -> 111 us
    pallas_call x1, Pallas kernels: 111 us -> 105 us  [local(): pl.pallas_call(functools.partial(block_kernel, (side, chans, n_img, real_...]
    pallas_call x1, Pallas kernels: 8.58 us -> 6.29 us  [local(): pl.pallas_call(functools.partial(finish_kernel, (chans, heads)), out_shap...]
where the time goes in v3:
time: 114 us
  Pallas kernels  111 us (97%)
  between operations  1.51 us (1%)
    pallas_call x1, Pallas kernels, local(): pl.pallas_call(functools.partial(block_kernel, (side, chans, n_img, real_...  105 us
    pallas_call x1, Pallas kernels, local(): pl.pallas_call(functools.partial(finish_kernel, (chans, heads)), out_shap...  6.29 us

profile of v3, /device:TPU:0, one launch (start us, length us, event | category | flops | bytes accessed | tf_op | source)
XLA Modules:
  0.0 113.5 jit_solution(5373379465193612702)
XLA Ops:
  1.4 0.6 divide_multiply_fusion.refs_12_
  2.0 105.1 %block.1 = (bf16[512,384]{1,0:T(8,128)(2,1)S(1)}, bf16[512,384]{1,0:T(8,128)(2,1)S(1)}, bf16[2,5376,128]{2,1,0:T(8,128)(2,1)S(1)}, bf16[2,5376,128]{2,1,0:T(8,12...) custom-call(bf16[512,384]{1,0:T(8,128)(2,1)} %bitcast.13, bf16[512,384]{1,0:T(8,128)(2,1)} %bitcast.14, ...), custom_call_target="tpu_custom_call" | custom-call | flops 20000000000 | bytes 20000000 | tf_op jit(solution)/shard_map/block/pallas_call | solution.py:958
  107.1 6.3 %finish.1 = (bf16[512,384]{1,0:T(8,128)(2,1)}, bf16[512,384]{1,0:T(8,128)(2,1)}, f32[384]{0:T(512)}, f32[384]{0:T(512)}, f32[3456,384]{1,0:T(8,128)}, /*index=5*...) custom-call(bf16[2,5376,128]{2,1,0:T(8,128)(2,1)S(1)} %get-tuple-ele, ...), custom_call_target="tpu_custom_call" | custom-call | flops 100000000 | bytes 23000000 | tf_op jit(solution)/shard_map/finish/pallas_call | solution.py:981
  (3 shorter events, 0.1 us)

commit v4 on v3

--- a/solution.py
+++ b/solution.py
@@ -21,15 +21,15 @@
 MC = 512
 TC = 256
 X_FIRST, Y_FIRST, Z_FIRST = (0, 1, 2, 3), (1, 2, 0, 3), (2, 0, 1, 3)
-KERNEL_FLOWS = ((X_FIRST, 4), (Y_FIRST, 4), (Z_FIRST, 4), (X_FIRST, 3), (Y_FIRST, 3), (Z_FIRST, 3))
+KERNEL_FLOWS = ((Z_FIRST, 4), (X_FIRST, 4), (Y_FIRST, 4), (Z_FIRST, 3), (X_FIRST, 3), (Y_FIRST, 3))
 PROJECT_FLOWS = ((X_FIRST, 3), (Y_FIRST, 3), (Z_FIRST, 3))
 SECOND, FIRST, PROJECT = tuple(range(16)), tuple(range(16, 32)), tuple(range(32, 48))
 PLAN = (
     (),
     SECOND,
     (),
+    (),
     SECOND,
-    SECOND + PROJECT,
     SECOND + FIRST + PROJECT,
     (),
     SECOND + FIRST + PROJECT,
@@ -184,12 +184,13 @@
 def block_kernel(dims, *refs):
     side, chans, n_img, real_k, real_p, bits, flow_sems = dims
     (
-        x_in, g_in, ext, p_g1, p_s1, p_o1, p_g2, p_s2, p_o2, p_g3, p_s3, p_oo, t_act, e_off, off_in, k1_h, k2_h, wi_h, wo_h, ew_h,
+        x_in, g_in, ext, h_g1, h_s1, h_o1, h_g2, h_s2, h_o2, h_g3, h_s3, h_oo, h_t, h_eo, h_oi, k1_h, k2_h, wi_h, wo_h, ew_h,
         res_v, ing_v, out1, out2, outp, vall,
         k1, k2, wo, ew, wq, xw, gf, mask, film, act1, act2, act3, dd2, dd1,
         cv, hid, tmp, resid, qa, ka, va, kat, vat, dot_t, att_t, dqkv,
         tsum, trecv, datt_s, datt_r, dm, act_t1, act_t2, act_t3, ing_r,
         pay1, pay2, payp, rb1, rb2, rbp, vx, vr,
+        p_g1, p_s1, p_o1, p_g2, p_s2, p_o2, p_g3, p_s3, p_oo, t_act, e_off, off_in,
         lsem, xs, xr, fs, fr,
     ) = refs
     img = lax.axis_index("img")
@@ -231,10 +232,22 @@
     other_rows = pl.ds(aligned(half * oc, half), half)
     copies = (
         (x_in.at[:, win], xw.at[my_rows]),
+        (wi_h, dqkv.at[pl.ds(0, chans)]),
+        (h_g1, p_g1),
+        (h_s1, p_s1),
+        (h_o1, p_o1),
+        (h_g2, p_g2),
+        (h_s2, p_s2),
+        (h_o2, p_o2),
+        (h_g3, p_g3),
+        (h_s3, p_s3),
+        (h_oo, p_oo),
+        (h_t, t_act),
+        (h_eo, e_off),
+        (h_oi, off_in),
+        (ew_h, ew),
         (k1_h, k1),
         (g_in, gf.at[my_rows]),
-        (ew_h, ew),
-        (wi_h, dqkv.at[pl.ds(0, chans)]),
         (wo_h, wo.at[pl.ds(0, chans)]),
         (k2_h, k2),
     )
@@ -242,18 +255,7 @@
         cp = pltpu.make_async_copy(src, dst, lsem.at[k])
         cp.start()
         loads.append(cp)
-    load_x, load_k1, load_g, load_ew, load_wi, load_wo, load_k2 = loads
-    pl.semaphore_wait(barrier, len(peers))
-
-    def swap(src, dst, k):
-        cp = pltpu.make_async_remote_copy(
-            src_ref=src, dst_ref=dst, send_sem=xs.at[k], recv_sem=xr.at[k], device_id=(img, oc), device_id_type=MESH
-        )
-        cp.start()
-        return cp
-
-    swap_x = swap(x_in.at[:, owin], xw.at[my_rows], 0)
-    swap_g = swap(g_in, gf.at[my_rows], 1)
+    load_x, load_wi, *small, load_ew, load_k1, load_g, load_wo, load_k2 = loads
 
     lane = lax.broadcasted_iota(jnp.int32, (1, WIN), 1)
     own_f = (jnp.where(first, lane, WIN - 1 - lane) < own_chans).astype(F32)
@@ -264,13 +266,6 @@
     gi = lax.broadcasted_iota(jnp.int32, (WIN, WIN), 0) + LANES * c
     gj = lax.broadcasted_iota(jnp.int32, (WIN, WIN), 1) + LANES * c
     same = (gi // per == gj // per).astype(F32).astype(BF)
-
-    def pvec(ref):
-        return ref[win].reshape(1, WIN)
-
-    gain1, shift1, offset1 = pvec(p_g1), pvec(p_s1), pvec(p_o1)
-    gain2, shift2, offset2 = pvec(p_g2), pvec(p_s2), pvec(p_o2)
-    gain3, shift3 = pvec(p_g3), pvec(p_s3)
 
     def group_totals(a, b):
         both = jnp.concatenate([a, b], axis=0)
@@ -317,6 +312,47 @@
     att_t[pl.ds(own_chans, WIN - own_chans), :] = jnp.zeros((WIN - own_chans, px), BF)
     vx[...] = jnp.zeros(vx.shape, F32)
 
+    pl.semaphore_wait(barrier, len(peers))
+
+    def swap(src, dst, k):
+        cp = pltpu.make_async_remote_copy(
+            src_ref=src, dst_ref=dst, send_sem=xs.at[k], recv_sem=xr.at[k], device_id=(img, oc), device_id_type=MESH
+        )
+        cp.start()
+        return cp
+
+    swap_x = swap(x_in.at[:, owin], xw.at[my_rows], 0)
+    swap_g = swap(g_in, gf.at[my_rows], 1)
+
+    lane1 = lax.broadcasted_iota(jnp.int32, (1, LANES), 1)
+    low1 = lane1 < HEAD_DIM
+    load_wi.wait()
+    for k in range(3 * heads):
+        place = 3 * heads * c + k
+        blk = dqkv[pl.ds(0, chans), pl.ds(aligned((place // 2) * LANES, LANES), LANES)].astype(F32)
+        blk = jnp.where(place % 2 == 0, blk, pltpu.roll(blk, HEAD_DIM, 1))
+        wq[:, pl.ds(k * LANES, LANES)] = jnp.where(low1, blk, 0.0).astype(BF)
+
+    for cp in small:
+        cp.wait()
+
+    def pvec(ref):
+        return ref[win].reshape(1, WIN)
+
+    gain1, shift1, offset1 = pvec(p_g1), pvec(p_s1), pvec(p_o1)
+    gain2, shift2, offset2 = pvec(p_g2), pvec(p_s2), pvec(p_o2)
+    gain3, shift3 = pvec(p_g3), pvec(p_s3)
+
+    load_ew.wait()
+    t = t_act[...]
+    t_a = t.astype(BF).astype(F32)
+    t_b = (t - t_a).astype(BF).astype(F32)
+    row16 = lax.broadcasted_iota(jnp.int32, (16, t.shape[1]), 0)
+    t_rows = jnp.where(row16 == 0, t_a, jnp.where(row16 == 1, t_b, jnp.where(row16 == 2, t - t_a - t_b, 0.0)))
+    film[...] = total(dot(t_rows.astype(BF), ew[...])) + e_off[...].reshape(1, -1)
+    scale2 = 1.0 + film[:, win]
+    move2 = film[:, pl.ds(aligned(chans + LANES * c, LANES), WIN)]
+
     def stats_step(v, m, carry):
         vm = v * m
         return carry[0] + fold(vm), carry[1] + fold(vm * v)
@@ -387,26 +423,7 @@
         cv[rows_at(j, MC), :] = conv(act1, c, k1, False, j)
         return 0
 
-    lax.fori_loop(0, px // MC, body, 0)
-    lane1 = lax.broadcasted_iota(jnp.int32, (1, LANES), 1)
-    low1 = lane1 < HEAD_DIM
-    load_wi.wait()
-    for k in range(3 * heads):
-        place = 3 * heads * c + k
-        blk = dqkv[pl.ds(0, chans), pl.ds(aligned((place // 2) * LANES, LANES), LANES)].astype(F32)
-        blk = jnp.where(place % 2 == 0, blk, pltpu.roll(blk, HEAD_DIM, 1))
-        wq[:, pl.ds(k * LANES, LANES)] = jnp.where(low1, blk, 0.0).astype(BF)
-
-    load_ew.wait()
-    t = t_act[...]
-    t_a = t.astype(BF).astype(F32)
-    t_b = (t - t_a).astype(BF).astype(F32)
-    row16 = lax.broadcasted_iota(jnp.int32, (16, t.shape[1]), 0)
-    t_rows = jnp.where(row16 == 0, t_a, jnp.where(row16 == 1, t_b, jnp.where(row16 == 2, t - t_a - t_b, 0.0)))
-    film[...] = total(dot(t_rows.astype(BF), ew[...])) + e_off[...].reshape(1, -1)
-    scale2 = 1.0 + film[:, win]
-    move2 = film[:, pl.ds(aligned(chans + LANES * c, LANES), WIN)]
-
+    lax.fori_loop(0, px // MC, body, 0, unroll=True)
     swap_a1.wait()
 
     def body(j, carry):
@@ -414,7 +431,7 @@
         cv[rows_at(j, MC), :] = v
         return stats_step(v, mask2(j, MC), carry)
 
-    mean2, rstd2 = moments(lax.fori_loop(0, px // MC, body, (zero8, zero8)))
+    mean2, rstd2 = moments(lax.fori_loop(0, px // MC, body, (zero8, zero8), unroll=True))
     mul2 = rstd2 * gain2 * scale2
     add2 = (shift2 - mean2 * rstd2 * gain2) * scale2 + move2
 
@@ -433,7 +450,7 @@
         hid[at, :] = conv(act2, c, k2, False, j) + offset2 + xw[at, :].astype(F32)
         return 0
 
-    lax.fori_loop(0, px // MC, body, 0)
+    lax.fori_loop(0, px // MC, body, 0, unroll=True)
     swap_a2.wait()
 
     def body(j, carry):
@@ -441,7 +458,7 @@
         hid[rows_at(j, MC), :] = v
         return stats_step(v, mask2(j, MC), carry)
 
-    mean3, rstd3 = moments(lax.fori_loop(0, px // MC, body, (zero8, zero8)))
+    mean3, rstd3 = moments(lax.fori_loop(0, px // MC, body, (zero8, zero8), unroll=True))
     mul3 = rstd3 * gain3
     add3 = shift3 - mean3 * mul3
 
@@ -470,7 +487,7 @@
             dot_t[h, pl.ds(0, HEAD_DIM), rows_at(j, MC)] = o[HEAD_DIM * h : HEAD_DIM * (h + 1)].astype(BF)
         return 0
 
-    lax.fori_loop(0, px // MC, body, 0)
+    lax.fori_loop(0, px // MC, body, 0, unroll=True)
 
     turn(act1, side, act_t1)
     turn(act2, side, act_t2)
@@ -494,7 +511,7 @@
             vat[h, :, at] = v.T.astype(BF)
         return 0
 
-    lax.fori_loop(0, px // MC, body, 0)
+    lax.fori_loop(0, px // MC, body, 0, unroll=True)
 
     row128 = lax.broadcasted_iota(jnp.int32, (LANES, px), 0)
 
@@ -524,7 +541,7 @@
         datt_s[at, :] = dot_nt(dqkv[at, :], wq[owin, :]).astype(BF)
         return 0
 
-    lax.fori_loop(0, px // MC, body, 0)
+    lax.fori_loop(0, px // MC, body, 0, unroll=True)
     swap_da = swap(datt_s, datt_r, 5)
 
     def body(j, _):
@@ -532,7 +549,7 @@
         tmp[at, :] = dot_nt(dqkv[at, :], wq[win, :])
         return 0
 
-    lax.fori_loop(0, px // MC, body, 0)
+    lax.fori_loop(0, px // MC, body, 0, unroll=True)
     turn(act3, 0, act_t3)
 
     used = [0]
@@ -650,7 +667,7 @@
         tmp[at, :] = u
         return back_sums(carry, u, (cv[at, :] - mean2) * rstd2)
 
-    s0, s1 = lax.fori_loop(0, px // MC, body, (zero8, zero8))
+    s0, s1 = lax.fori_loop(0, px // MC, body, (zero8, zero8), unroll=True)
     advance(0)
     t0, t1 = total(s0), total(s1)
     vx[pl.ds(9, 1), win] = (gain2 * t1 + shift2 * t0) * own_f
@@ -719,7 +736,7 @@
         tmp[at, :] = u
         return back_sums(carry, u, (x - mean1) * rstd1)
 
-    s0, s1 = lax.fori_loop(0, px // MC, body, (zero8, zero8))
+    s0, s1 = lax.fori_loop(0, px // MC, body, (zero8, zero8), unroll=True)
     advance(5)
     vx[pl.ds(0, 1), win] = total(s1) * own_f
     vx[pl.ds(1, 1), win] = total(s0) * own_f
@@ -952,7 +969,8 @@
         V((rows_k, LANES), BF), V((rows_k, LANES), BF), V((rows_p, LANES), BF),
         V((rows_k, LANES), BF), V((rows_k, LANES), BF), V((rows_p, LANES), BF),
         V((16, chans), F32), V((16, chans), F32),
-        pltpu.SemaphoreType.DMA((7,)), pltpu.SemaphoreType.DMA((11,)), pltpu.SemaphoreType.DMA((11,)),
+        V((chans,), F32), V((chans,), F32), V((chans,), F32), V((chans,), F32), V((chans,), F32), V((chans,), F32), V((chans,), F32), V((chans,), F32), V((chans,), F32), V((1, 2 * chans), F32), V((2 * chans,), F32), V((2 * chans,), F32),
+        pltpu.SemaphoreType.DMA((19,)), pltpu.SemaphoreType.DMA((11,)), pltpu.SemaphoreType.DMA((11,)),
         pltpu.SemaphoreType.DMA((n_sem,)), pltpu.SemaphoreType.DMA((n_sem,)),
     ]
     res, ing, pk1, pk2, pp, vec = pl.pallas_call(
@@ -961,7 +979,7 @@
             V((half, chans), BF), V((half, chans), BF), V((2, rows_k, LANES), BF), V((2, rows_k, LANES), BF),
             V((2, rows_p, LANES), BF), V((n_img, 16, chans), F32),
         ),
-        in_specs=[anym, anym, smem] + [vm] * 12 + [anym, anym, anym, anym, anym],
+        in_specs=[anym, anym, smem] + [anym] * 12 + [anym, anym, anym, anym, anym],
         out_specs=(vm,) * 6,
         scratch_shapes=scratch,
         compiler_params=pltpu.CompilerParams(collective_id=0, has_side_effects=True, vmem_limit_bytes=50 * 2**20),

time: 114 us -> 108 us (0.947)
  Pallas kernels: 111 us -> 106 us
    pallas_call x1, Pallas kernels: 105 us -> 99.4 us  [local(): pl.pallas_call(functools.partial(block_kernel, (side, chans, n_img, real_...]
where the time goes in v4:
time: 108 us
  Pallas kernels  106 us (98%)
  between operations  1.53 us (1%)
    pallas_call x1, Pallas kernels, local(): pl.pallas_call(functools.partial(block_kernel, (side, chans, n_img, real_...  99.4 us
    pallas_call x1, Pallas kernels, local(): pl.pallas_call(functools.partial(finish_kernel, (chans, heads)), out_shap...  6.29 us

profile of v4, /device:TPU:0, one launch (start us, length us, event | category | flops | bytes accessed | tf_op | source)
XLA Modules:
  0.0 107.9 jit_solution(939787661930438)
XLA Ops:
  1.4 0.6 divide_multiply_fusion.refs_12_
  2.0 99.4 %block.1 = (bf16[512,384]{1,0:T(8,128)(2,1)S(1)}, bf16[512,384]{1,0:T(8,128)(2,1)S(1)}, bf16[2,5376,128]{2,1,0:T(8,128)(2,1)S(1)}, bf16[2,5376,128]{2,1,0:T(8,12...) custom-call(bf16[512,384]{1,0:T(8,128)(2,1)} %bitcast.13, bf16[512,384]{1,0:T(8,128)(2,1)} %bitcast.14, ...), custom_call_target="tpu_custom_call" | custom-call | flops 20000000000 | bytes 20000000 | tf_op jit(solution)/shard_map/block/pallas_call | solution.py:976
  101.4 6.3 %finish.1 = (bf16[512,384]{1,0:T(8,128)(2,1)}, bf16[512,384]{1,0:T(8,128)(2,1)}, f32[384]{0:T(512)}, f32[384]{0:T(512)}, f32[3456,384]{1,0:T(8,128)}, /*index=5*...) custom-call(bf16[2,5376,128]{2,1,0:T(8,128)(2,1)S(1)} %get-tuple-ele, ...), custom_call_target="tpu_custom_call" | custom-call | flops 100000000 | bytes 23000000 | tf_op jit(solution)/shard_map/finish/pallas_call | solution.py:999
  (3 shorter events, 0.1 us)
